TPU v7x, 512 devices: a whole 4x4x16 slice. The times are simulated.
512 devices in a mesh: wide: 128 (over z, x, core), narrow: 4 (over y).
Axes of the slice: x: 4, y: 4, z: 16, core: 2. Of those that a mesh axis runs over, the one named last changes fastest.
Arguments:
- state: float32 [2, 33554432], P(None, ('wide', 'narrow')), may hold values from -6 to 6
- gates: float32 [8, 2, 128, 128], replicated, may hold values from -1 to 1, as said below
- gate_qubits: int32 [8, 7], replicated, may hold values from 7 to 15, as said below
- swap_order: int32 [9], replicated, may hold values from 7 to 15, as said below
Outputs:
- checkpoint: float32 [2, 33554432], P(None, ('wide', 'narrow'))
Inputs may be any that keep to these rules, and one draw needn't show every extreme that they name: `gate_qubits`: each row names 7 different qubits. `swap_order`: each number of the range appears once. Each gates[g, 0] + i gates[g, 1] is a unitary matrix.
All inputs are finite; a program needn't handle non-finite values.
Results may differ from a plain program's by a relative error of at most 0.0003.
Values sent between devices are 32-bit elements; how exact they have to be, the bound alone decides.
No kernel may reach another device: no remote copies, remote signals or barrier semaphores. Data moves between devices by JAX's collectives and lax.ppermute only.
A program may use at most 64 MiB of HBM per device.

v0:
```python
import math

import jax
import jax.numpy as jnp
from jax import lax
from jax.sharding import Mesh
from jax.sharding import PartitionSpec as P

LANE_QUBITS = 7
WIDE = ("wide_0", "wide_1", "wide_2")
WIDE_NARROW = ("wide_0", "wide_1", "wide_2", "narrow")


companding = 16.0
companding_norm = math.log(16.0 + math.sqrt(257.0))


def over_axes(shard, axes):
    for axis in axes:
        shard = lax.pmax(shard, axis)
    return shard


def inverse_sinh(values):
    magnitude = jnp.abs(values)
    squared = magnitude * magnitude
    return jnp.sign(values) * jnp.log1p(magnitude + squared / (1.0 + jnp.sqrt(squared + 1.0)))


def shuffle_index(source, target, qubit_count):
    position = jnp.argsort(source)
    shifts = position[target]
    low_count = qubit_count // 2
    high_count = qubit_count - low_count
    low_values = jnp.arange(2**low_count, dtype=jnp.int32)
    high_values = jnp.arange(2**high_count, dtype=jnp.int32)
    low_bits = (
        jnp.right_shift(low_values[:, None], jnp.arange(low_count, dtype=jnp.int32)[None, :]) & 1
    )
    high_bits = (
        jnp.right_shift(high_values[:, None], jnp.arange(high_count, dtype=jnp.int32)[None, :]) & 1
    )
    low_part = jnp.sum(jnp.left_shift(low_bits, shifts[None, :low_count]), axis=1)
    high_part = jnp.sum(jnp.left_shift(high_bits, shifts[None, low_count:]), axis=1)
    return (high_part[:, None] + low_part[None, :]).reshape(-1)


def top_order(chosen, qubit_count):
    ranking = jnp.arange(qubit_count, dtype=jnp.int32)
    ranking = ranking.at[chosen].set(qubit_count + jnp.arange(chosen.shape[0], dtype=jnp.int32))
    return jnp.argsort(ranking)


def gate_blocks(matrix):
    real_part = matrix[0]
    imag_part = matrix[1]
    return jnp.stack([jnp.stack([real_part, imag_part]), jnp.stack([-imag_part, real_part])])


def apply_top(rows_view, matrix):
    gate_size = matrix.shape[-1]
    shaped = rows_view.reshape(2, gate_size, -1)
    mixed = jnp.einsum(
        "cbr,cdab->dar", shaped, gate_blocks(matrix), precision=lax.Precision.HIGHEST
    )
    return mixed.reshape(rows_view.shape)


def relayout(rows_view, layout, target, upper_count):
    return jnp.take(rows_view, shuffle_index(layout, target, upper_count), axis=1)


def local(state, gates, gate_qubits, swap_order):
    wide_count = lax.axis_size(WIDE)
    narrow_count = lax.axis_size("narrow")
    wide_bits = wide_count.bit_length() - 1
    narrow_bits = narrow_count.bit_length() - 1
    qubit_count = state.shape[1].bit_length() - 1
    upper_count = qubit_count - LANE_QUBITS
    lane_width = 2**LANE_QUBITS
    natural = jnp.arange(upper_count, dtype=jnp.int32)
    relative_gates = gate_qubits - LANE_QUBITS
    relative_swaps = swap_order - LANE_QUBITS
    amplitudes = state.reshape(2, -1, lane_width)
    layout = natural
    for number in range(3):
        target = top_order(relative_gates[number], upper_count)
        amplitudes = apply_top(relayout(amplitudes, layout, target, upper_count), gates[number])
        layout = target
    target = top_order(relative_swaps[upper_count - wide_bits :], upper_count)
    amplitudes = relayout(amplitudes, layout, target, upper_count)
    layout = target
    blocks = amplitudes.reshape(2, wide_count, -1)
    amplitudes = lax.all_to_all(blocks, WIDE, split_axis=1, concat_axis=1, tiled=True).reshape(
        2, -1, lane_width
    )
    for number in range(3, 6):
        target = top_order(relative_gates[number], upper_count)
        amplitudes = apply_top(relayout(amplitudes, layout, target, upper_count), gates[number])
        layout = target
    target = top_order(relative_swaps[:narrow_bits], upper_count)
    amplitudes = relayout(amplitudes, layout, target, upper_count)
    layout = target
    blocks = amplitudes.reshape(2, narrow_count, -1)
    amplitudes = lax.all_to_all(blocks, "narrow", split_axis=1, concat_axis=1, tiled=True).reshape(
        2, -1, lane_width
    )
    for number in range(6, 8):
        target = top_order(relative_gates[number], upper_count)
        amplitudes = apply_top(relayout(amplitudes, layout, target, upper_count), gates[number])
        layout = target
    final = relayout(amplitudes, layout, natural, upper_count).reshape(2, -1)
    local_high = jnp.max(final)
    local_low = jnp.min(final)
    extremes_pair = (over_axes(local_high, WIDE_NARROW), over_axes(-local_low, WIDE_NARROW))
    highest = extremes_pair[0]
    lowest = -extremes_pair[1]
    middle = (highest + lowest) * 0.5
    halfwidth = (highest - lowest) * 0.5 + 1e-06
    return inverse_sinh(companding * (final - middle) / halfwidth) / companding_norm


def solution(mesh):
    split = Mesh(
        mesh.devices.reshape(16, 4, 2, mesh.shape["narrow"]),
        ("wide_0", "wide_1", "wide_2", "narrow"),
    )
    return jax.shard_map(
        local,
        mesh=split,
        in_specs=(P(None, WIDE_NARROW), P(), P(), P()),
        out_specs=P(None, WIDE_NARROW),
        check_vma=False,
    )
```

profile of v0, /device:TPU:1, one launch (start us, length us, event | category | flops | bytes accessed | tf_op | source)
XLA Modules:
  0.0 204.2 jit_solution(17004490077611230294)
XLA Ops:
  22.8 2.1 %gather_fusion.11 = f32[512,2,128]{2,1,0:T(2,128)S(1)} fusion(f32[2,512,128]{2,0,1:T(2,128)S(1)} %bitcast.227, s32[1024]{0:T(1024)S(1)} %pad_clamp_fusion.10), kind=kCustom, calls=%fused_computation.clone | custom fusion | bytes 1050624 | tf_op jit(solution)/shard_map/jit(_take)/gather | solution.py:70
  24.9 1.8 select_bitcast_fusion.7
  28.8 2.1 %gather_fusion.12 = f32[512,2,128]{2,1,0:T(2,128)S(1)} fusion(f32[2,512,128]{2,0,1:T(2,128)S(1)} %copy.98, s32[1024]{0:T(1024)S(1)} %pad_clamp_fusion.9), kind=kCustom, calls=%fused_computation.1.clone | custom fusion | bytes 1050624 | tf_op jit(solution)/shard_map/jit(_take)/gather | solution.py:70
  30.9 1.8 select_bitcast_fusion.6
  33.9 2.1 %gather_fusion.13 = f32[512,2,128]{2,1,0:T(2,128)S(1)} fusion(f32[2,512,128]{2,0,1:T(2,128)S(1)} %copy.100, s32[1024]{0:T(1024)S(1)} %pad_clamp_fusion.8), kind=kCustom, calls=%fused_computation.2.clone | custom fusion | bytes 1050624 | tf_op jit(solution)/shard_map/jit(_take)/gather | solution.py:70
  36.0 1.8 select_bitcast_fusion.5
  39.0 2.1 %gather_fusion.14 = f32[512,2,128]{2,1,0:T(2,128)S(1)} fusion(f32[2,512,128]{2,0,1:T(2,128)S(1)} %copy.102, s32[1024]{0:T(1024)S(1)} %pad_clamp_fusion.7), kind=kCustom, calls=%fused_computation.3.clone | custom fusion | bytes 1050624 | tf_op jit(solution)/shard_map/jit(_take)/gather | solution.py:70
  41.1 2.5 %broadcast_select_fusion.2 = f32[512,2,128]{2,1,0:T(2,128)} fusion(f32[512,2,128]{2,1,0:T(2,128)S(1)} %gather_fusion.14, pred[512]{0:T(512)(128)(4,1)S(1)} %copy-done.9), kind=kLoop, calls=%fused_computation.62 | loop fusion | flops 131072 | bytes 1049088 | tf_op jit(solution)/shard_map/jit(_take)/select_n | solution.py:70
  43.6 20.5 %all-to-all-start = ((f32[2,128,512]{2,0,1:T(2,128)}), f32[2,128,512]{2,0,1:T(2,128)S(1)}, u32[]{:S(2)}, u32[]{:S(2)}) async-start(f32[2,128,512]{2,0,1:T(2,128)} %bitcast.67), calls=%async_computation | async-start | bytes 1048576 | tf_op jit(solution)/shard_map/all_to_all | solution.py:94
  76.0 1.3 sort.310
  94.0 1.3 sort.317
  96.7 2.1 %gather_fusion.15 = f32[512,2,128]{2,1,0:T(2,128)S(1)} fusion(f32[2,512,128]{2,0,1:T(2,128)S(1)} %bitcast.228, s32[1024]{0:T(1024)S(1)} %pad_clamp_fusion.6), kind=kCustom, calls=%fused_computation.4.clone | custom fusion | bytes 1050624 | tf_op jit(solution)/shard_map/jit(_take)/gather | solution.py:70
  98.8 1.8 select_bitcast_fusion.4
  101.8 2.1 %gather_fusion.16 = f32[512,2,128]{2,1,0:T(2,128)S(1)} fusion(f32[2,512,128]{2,0,1:T(2,128)S(1)} %copy.108, s32[1024]{0:T(1024)S(1)} %pad_clamp_fusion.5), kind=kCustom, calls=%fused_computation.5.clone | custom fusion | bytes 1050624 | tf_op jit(solution)/shard_map/jit(_take)/gather | solution.py:70
  103.9 1.8 select_bitcast_fusion.3
  106.8 2.1 %gather_fusion.17 = f32[512,2,128]{2,1,0:T(2,128)S(1)} fusion(f32[2,512,128]{2,0,1:T(2,128)S(1)} %copy.110, s32[1024]{0:T(1024)S(1)} %pad_clamp_fusion.4), kind=kCustom, calls=%fused_computation.6.clone | custom fusion | bytes 1050624 | tf_op jit(solution)/shard_map/jit(_take)/gather | solution.py:70
  108.9 1.8 select_bitcast_fusion.2
  111.9 2.1 %gather_fusion.18 = f32[512,2,128]{2,1,0:T(2,128)S(1)} fusion(f32[2,512,128]{2,0,1:T(2,128)S(1)} %copy.112, s32[1024]{0:T(1024)S(1)} %pad_clamp_fusion.3), kind=kCustom, calls=%fused_computation.7.clone | custom fusion | bytes 1050624 | tf_op jit(solution)/shard_map/jit(_take)/gather | solution.py:70
  114.0 2.5 %broadcast_select_fusion.1 = f32[512,2,128]{2,1,0:T(2,128)} fusion(f32[512,2,128]{2,1,0:T(2,128)S(1)} %gather_fusion.18, pred[512]{0:T(512)(128)(4,1)S(1)} %compare_and_fusion.3), kind=kLoop, calls=%fused_computation.61 | loop fusion | flops 131072 | bytes 1049088 | tf_op jit(solution)/shard_map/jit(_take)/select_n | solution.py:70
  116.5 4.2 %all-to-all-start.1 = ((f32[2,4,16384]{2,0,1:T(2,128)}), f32[2,4,16384]{2,0,1:T(2,128)S(1)}, u32[]{:S(2)}, u32[]{:S(2)}) async-start(f32[2,4,16384]{2,0,1:T(2,128)} %bitcast.79), calls=%async_computation.1 | async-start | bytes 1048576 | tf_op jit(solution)/shard_map/all_to_all | solution.py:105
  120.7 8.0 %all-to-all-done.1 = f32[2,4,16384]{2,0,1:T(2,128)S(1)} async-done(((f32[2,4,16384]{2,0,1:T(2,128)}), f32[2,4,16384]{2,0,1:T(2,128)S(1)}, u32[]{:S(2)}, u32[]{:S(2)}) %all-to-all-start.1) | async-done | bytes 524320 | tf_op jit(solution)/shard_map/all_to_all | solution.py:105
  128.7 2.1 %gather_fusion.19 = f32[512,2,128]{2,1,0:T(2,128)S(1)} fusion(f32[2,512,128]{2,0,1:T(2,128)S(1)} %bitcast.229, s32[1024]{0:T(1024)S(1)} %pad_clamp_fusion.2), kind=kCustom, calls=%fused_computation.8.clone | custom fusion | bytes 1050624 | tf_op jit(solution)/shard_map/jit(_take)/gather | solution.py:70
  130.8 1.8 select_bitcast_fusion.1
  133.8 2.1 %gather_fusion.20 = f32[512,2,128]{2,1,0:T(2,128)S(1)} fusion(f32[2,512,128]{2,0,1:T(2,128)S(1)} %copy.118, s32[1024]{0:T(1024)S(1)} %pad_clamp_fusion.1), kind=kCustom, calls=%fused_computation.9.clone | custom fusion | bytes 1050624 | tf_op jit(solution)/shard_map/jit(_take)/gather | solution.py:70
  135.8 1.8 select_bitcast_fusion
  138.8 2.1 %gather_fusion.21 = f32[512,2,128]{2,1,0:T(2,128)S(1)} fusion(f32[2,512,128]{2,0,1:T(2,128)S(1)} %copy.120, s32[1024]{0:T(1024)S(1)} %pad_clamp_fusion), kind=kCustom, calls=%fused_computation.10.clone | custom fusion | bytes 1050624 | tf_op jit(solution)/shard_map/jit(_take)/gather | solution.py:70
  140.9 2.4 %bitcast_reduce_fusion = (f32[]{:T(128)}, f32[]{:T(128)}, f32[512,2,128]{2,1,0:T(2,128)S(1)}) fusion(f32[512,2,128]{2,1,0:T(2,128)S(1)} %gather_fusion.21, pred[512]{0:T(512)(128)(4,1)S(1)} %compare_and_fusion), kind=kLoop, calls=%fused_computation.48 | loop fusion | flops 393214 | bytes 1049096 | tf_op jit(solution)/shard_map/reduce_min | solution.py:114
  143.9 25.7 %all-reduce = (f32[]{:T(128)}, f32[]{:T(128)}) all-reduce(f32[]{:T(128)} %get-tuple-element.49, f32[]{:T(128)S(6)} %neg.94), channel_id=1, replica_groups=mesh['wide_0'=16,'wide_1'=4,'wide_2'=2,'narrow'=4] {'wide_0'}, use_global_device_ids=true, to_apply=%region_54.56 | all-reduce | flops 2 | bytes 16 | tf_op jit(solution)/shard_map/pmax | solution.py:20
  169.6 9.0 %all-reduce.2 = (f32[]{:T(128)}, f32[]{:T(128)}) all-reduce(f32[]{:T(128)} %get-tuple-element.50, f32[]{:T(128)} %get-tuple-element.51), channel_id=1, replica_groups=mesh['wide_0'=16,'wide_1'=4,'wide_2'=2,'narrow'=4] {'wide_1'}, use_global_device_ids=true, to_apply=%region_55.57 | all-reduce | flops 2 | bytes 16 | tf_op jit(solution)/shard_map/pmax | solution.py:20
  178.6 13.1 %all-reduce.3 = (f32[]{:T(128)}, f32[]{:T(128)}) all-reduce(f32[]{:T(128)} %get-tuple-element.54, f32[]{:T(128)} %get-tuple-element.55), channel_id=1, replica_groups=mesh['wide_0'=16,'wide_1'=4,'wide_2'=2,'narrow'=4] {'wide_2'}, use_global_device_ids=true, to_apply=%region_56.58 | all-reduce | flops 2 | bytes 16 | tf_op jit(solution)/shard_map/pmax | solution.py:20
  191.7 7.5 %all-reduce.1 = (f32[]{:T(128)}, f32[]{:T(128)}) all-reduce(f32[]{:T(128)} %get-tuple-element.56, f32[]{:T(128)} %get-tuple-element.57), channel_id=1, replica_groups=mesh['wide_0'=16,'wide_1'=4,'wide_2'=2,'narrow'=4] {'narrow'}, use_global_device_ids=true, to_apply=%region_57.59 | all-reduce | flops 2 | bytes 16 | tf_op jit(solution)/shard_map/pmax | solution.py:20
  201.0 3.2 %fusion.3 = f32[2,65536]{1,0:T(2,128)} fusion(f32[512,2,128]{2,1,0:T(2,128)S(1)} %get-tuple-element.58, f32[]{:T(128)S(6)} %add.424, f32[]{:T(128)S(6)} %mul.22), kind=kLoop, calls=%fused_computation.46 | loop fusion | flops 1572864 | bytes 1048584 | tf_op jit(solution)/shard_map/div | solution.py:120
  (261 shorter events, 62.5 us)
Async XLA Ops:
  0.0 22.8 %copy-start = (f32[2,65536]{1,0:T(2,128)S(1)}, f32[2,65536]{1,0:T(2,128)}, u32[]{:S(2)}) copy-start(f32[2,65536]{1,0:T(2,128)} %param.6) | copy-start | bytes 1572868
  0.0 6.9 %copy-start.1 = (f32[8,2,128,128]{3,2,1,0:T(8,128)S(1)}, f32[8,2,128,128]{3,2,1,0:T(8,128)}, u32[]{:S(2)}) copy-start(f32[8,2,128,128]{3,2,1,0:T(8,128)} %param.7) | copy-start | bytes 3145732
  0.8 0.6 copy-start.10
  20.6 0.5 copy-start.12
  28.8 2.1 %copy-start.7 = (pred[512]{0:T(512)(128)(4,1)S(1)}, pred[512]{0:T(512)(128)(4,1)}, u32[]{:S(2)}) copy-start(pred[512]{0:T(512)(128)(4,1)} %compare_and_fusion.9) | copy-start | bytes 1540
  33.9 2.1 %copy-start.8 = (pred[512]{0:T(512)(128)(4,1)S(1)}, pred[512]{0:T(512)(128)(4,1)}, u32[]{:S(2)}) copy-start(pred[512]{0:T(512)(128)(4,1)} %compare_and_fusion.8) | copy-start | bytes 1540
  39.0 2.1 %copy-start.9 = (pred[512]{0:T(512)(128)(4,1)S(1)}, pred[512]{0:T(512)(128)(4,1)}, u32[]{:S(2)}) copy-start(pred[512]{0:T(512)(128)(4,1)} %compare_and_fusion.7) | copy-start | bytes 1540
  43.6 20.5 %copy-start.11 = (s32[9]{0:T(128)S(1)}, s32[9]{0:T(128)}, u32[]{:S(2)}) copy-start(s32[9]{0:T(128)} %copy-done.10) | copy-start | bytes 112
  43.6 53.1 %all-to-all-start = ((f32[2,128,512]{2,0,1:T(2,128)}), f32[2,128,512]{2,0,1:T(2,128)S(1)}, u32[]{:S(2)}, u32[]{:S(2)}) async-start(f32[2,128,512]{2,0,1:T(2,128)} %bitcast.67), calls=%async_computation | async-start | bytes 1048576 | tf_op jit(solution)/shard_map/all_to_all | solution.py:94
  64.2 0.6 copy-start.6
  66.7 0.6 copy-start.13
  69.7 0.7 copy-start.5
  74.8 0.6 copy-start.4
  84.1 0.6 copy-start.3
  89.1 0.6 copy-start.2
  116.5 12.2 %all-to-all-start.1 = ((f32[2,4,16384]{2,0,1:T(2,128)}), f32[2,4,16384]{2,0,1:T(2,128)S(1)}, u32[]{:S(2)}, u32[]{:S(2)}) async-start(f32[2,4,16384]{2,0,1:T(2,128)} %bitcast.79), calls=%async_computation.1 | async-start | bytes 1048576 | tf_op jit(solution)/shard_map/all_to_all | solution.py:105
where the time goes:
time: 205 us; the launch traced here: 204 us
  other arithmetic  60.6 us (30%)
  blocking collectives  55.3 us (27%)
  local copies, waits for them, and re-layouts  47.1 us (23%)
  starting transfers between devices  24.7 us (12%)
  waiting for transfers between devices  7.98 us (4%)
  matrix products  4.9 us (2%)
  between operations  3.67 us (2%)
    pmax x4, blocking collectives, over_axes(): shard = lax.pmax(shard, axis)  55.3 us
    gather x11, local copies, waits for them, and re-layouts, relayout(): jnp.take(rows_view, shuffle_index(layout, target, upper_count), axis=1)  22.8 us
    all_to_all x1, starting transfers between devices, local(): lax.all_to_all(blocks, WIDE, split_axis=1, concat_axis=1, tiled=True)  20.5 us
    select_n x21, other arithmetic, relayout(): jnp.take(rows_view, shuffle_index(layout, target, upper_count), axis=1)  19.1 us
    sort x11, other arithmetic, shuffle_index(): position = jnp.argsort(source)  14.4 us
    sort x10, other arithmetic, top_order(): return jnp.argsort(ranking)  13 us
    all_to_all x1, waiting for transfers between devices, local(): lax.all_to_all(blocks, 'narrow', split_axis=1, concat_axis=1, tiled=True)  7.98 us
    gather x11, local copies, waits for them, and re-layouts, shuffle_index(): shifts = position[target]  7.22 us
  transfers between devices with their start and end apart: 2, of which 1 were waited for; matrix products, arithmetic and copies ran while one was open for 14% of the time, Pallas kernels for 0%

commit v1 on v0

v1 whole, which is shorter than its diff:
```python
import functools
import math

import jax
import jax.numpy as jnp
from jax import lax
from jax.experimental import pallas as pl
from jax.experimental.pallas import tpu as pltpu
from jax.sharding import Mesh
from jax.sharding import PartitionSpec as P

LANE_QUBITS = 7
UPPER = 9
ROWS = 2**UPPER
DIM = 128
Z, XCY = "z", ("x", "core", "narrow")
ALL = ("z", "x", "core", "narrow")

F32, BF16, I32 = jnp.float32, jnp.bfloat16, jnp.int32
companding = 16.0
companding_norm = math.log(16.0 + math.sqrt(257.0))
VMEM_LIMIT = 40 * 2**20


def dot(a, b):
    return jnp.dot(a, b, preferred_element_type=F32)


def pieces(x):
    high = x.astype(BF16)
    return high, (x - high.astype(F32)).astype(BF16)


def gate_layout(gate_qubits, gate):
    chosen = [gate_qubits[gate, k] - LANE_QUBITS for k in range(7)]
    used = sum(lax.shift_left(I32(1), c) for c in chosen)
    low, high = I32(0), I32(0)
    for row_bit in range(UPPER):
        free = (lax.shift_right_logical(used, I32(row_bit)) & 1) == 0
        low = jnp.where(free & (high == 0) & (low == 0), row_bit + 100, low)
        high = jnp.where(free, row_bit, high)
    return chosen + [low - 100, high]


def swap_layout(swap_order):
    order = [swap_order[k] - LANE_QUBITS for k in range(UPPER)]
    return order[2:] + order[:2]


def permutation(source, target, place):
    if target is not None:
        for b in range(UPPER):
            place[target[b]] = I32(b)
    index = lax.broadcasted_iota(I32, (1, ROWS), 1)
    moved = jnp.zeros((1, ROWS), I32)
    for b in range(UPPER):
        row_bit = b if source is None else source[b]
        to = row_bit if target is None else place[row_bit]
        moved = moved + (lax.shift_right_logical(index, b) & 1) * lax.shift_left(I32(1), I32(to))
    rows = lax.broadcasted_iota(I32, (ROWS, ROWS), 0)
    return jnp.where(rows == moved, 1.0, 0.0).astype(BF16)


def gate_matrix(gates_ref, gate):
    real, imag = gates_ref[gate, 0], gates_ref[gate, 1]
    top = jnp.concatenate([real, -imag], axis=1)
    bottom = jnp.concatenate([imag, real], axis=1)
    high, low = pieces(jnp.concatenate([top, bottom], axis=0))
    return jnp.concatenate([high, low], axis=0)


def apply_gate(matrix, high, low):
    width = high.shape[1] // 2
    size = 2 * DIM
    done = []
    for other in range(ROWS // DIM):
        rows = slice(other * DIM, (other + 1) * DIM)
        stacked = jnp.concatenate([high[rows, :width], high[rows, width:]], axis=0)
        both = dot(matrix, stacked)
        mixed = both[:size] + both[size:]
        if low is not None:
            rest = jnp.concatenate([low[rows, :width], low[rows, width:]], axis=0)
            mixed = mixed + dot(matrix[:size], rest)
        done.append(jnp.concatenate([mixed[:DIM], mixed[DIM:]], axis=1))
    return jnp.concatenate(done, axis=0)


def permute(matrix, high, low):
    return dot(matrix, high).astype(BF16), dot(matrix, low).astype(BF16)


def quarters(slabs):
    lane = lax.broadcasted_iota(I32, slabs[0].shape, 1)
    first = lane < 64
    half = [None] * 4
    for i in range(2):
        half[i] = jnp.where(first, slabs[i], pltpu.roll(slabs[i + 2], 64, 1))
        half[i + 2] = jnp.where(first, pltpu.roll(slabs[i], 64, 1), slabs[i + 2])
    even = (lane & 32) == 0
    out = [None] * 4
    for i in (0, 2):
        out[i] = jnp.where(even, half[i], pltpu.roll(half[i + 1], 32, 1))
        out[i + 1] = jnp.where(even, pltpu.roll(half[i], 96, 1), half[i + 1])
    return out


def slabs_of(x):
    return [x[DIM * i : DIM * (i + 1)] for i in range(4)]


def first_kernel(gate_qubits, swap_order, state_ref, gates_ref, out_ref, place):
    planes = [state_ref[pl.ds(p, ROWS, stride=2), :] for p in range(2)]
    high, low = pieces(jnp.concatenate(planes, axis=1))
    layout = None
    for gate in range(3):
        target = gate_layout(gate_qubits, gate)
        high, low = permute(permutation(layout, target, place), high, low)
        layout = target
        high, low = pieces(apply_gate(gate_matrix(gates_ref, gate), high, low))
    matrix = permutation(layout, swap_layout(swap_order), place)
    mixed = dot(matrix, high) + dot(matrix, low)
    for p in range(2):
        for y, slab in enumerate(quarters(slabs_of(mixed[:, DIM * p : DIM * (p + 1)]))):
            out_ref[pl.ds(2 * y + p, DIM, stride=8), :] = slab


def compose_kernel(gate_qubits, swap_order, gates_ref, second_ref, third_ref, place):
    swapped = swap_layout(swap_order)
    for out_ref, numbers, last in ((second_ref, (3, 4, 5), swapped), (third_ref, (6, 7), None)):
        layout = swapped
        for gate in numbers:
            target = gate_layout(gate_qubits, gate)
            matrix = permutation(layout, target, place)
            if gate == numbers[0]:
                high = jnp.concatenate([matrix, jnp.zeros_like(matrix)], axis=1)
                low = None
            else:
                high, low = permute(matrix, high, low)
            layout = target
            high, low = pieces(apply_gate(gate_matrix(gates_ref, gate), high, low))
        high, low = permute(permutation(layout, last, place), high, low)
        for number, part in enumerate((high[:, :ROWS], high[:, ROWS:], low[:, :ROWS], low[:, ROWS:])):
            out_ref[ROWS * number : ROWS * (number + 1), :] = part


def apply_matrix(matrix_ref, real, imag):
    high, low = pieces(jnp.concatenate([real, imag], axis=1))
    both = dot(matrix_ref[...], high)
    total = both[: 2 * ROWS] + both[2 * ROWS :] + dot(matrix_ref[: 2 * ROWS, :], low)
    return (
        total[:ROWS, :DIM] - total[ROWS:, DIM:],
        total[ROWS:, :DIM] + total[:ROWS, DIM:],
    )


def middle_kernel(arrived_ref, second_ref, third_ref, out_ref, extremes_ref):
    planes = [
        jnp.concatenate(
            quarters([arrived_ref[pl.ds(2 * n + p, DIM, stride=8), :] for n in range(4)]), axis=0
        )
        for p in range(2)
    ]
    planes = apply_matrix(second_ref, *planes)
    planes = [jnp.concatenate(quarters(slabs_of(x)), axis=0) for x in planes]
    planes = apply_matrix(third_ref, *planes)
    highest = jnp.max(jnp.maximum(planes[0], planes[1]))
    lowest = jnp.min(jnp.minimum(planes[0], planes[1]))
    lane = lax.broadcasted_iota(I32, extremes_ref.shape, 1)
    extremes_ref[...] = jnp.where(lane < 64, highest, -lowest)
    for p in range(2):
        for t, slab in enumerate(quarters(slabs_of(planes[p]))):
            out_ref[t, p] = slab


def last_kernel(extremes_ref, arrived_ref, out_ref):
    lane = lax.broadcasted_iota(I32, extremes_ref.shape, 1)
    found = extremes_ref[...]
    least = jnp.min(found)
    highest = jnp.max(jnp.where(lane < 64, found, least))
    lowest = -jnp.max(jnp.where(lane < 64, least, found))
    middle = (highest + lowest) * 0.5
    halfwidth = (highest - lowest) * 0.5 + 1e-06
    for p in range(2):
        for q, slab in enumerate(quarters([arrived_ref[y, p] for y in range(4)])):
            value = companding * (slab - middle) / halfwidth
            size = jnp.abs(value)
            curve = jnp.log(size + jnp.sqrt(size * size + 1.0)) / companding_norm
            out_ref[pl.ds(2 * DIM * q + p, DIM, stride=2), :] = jnp.where(value < 0, -curve, curve)


def call(kernel, inputs, outs, places, scratch=(), flops=0, gates=False):
    return pl.pallas_call(
        kernel,
        out_shape=outs,
        in_specs=[pl.BlockSpec(memory_space=m) for m in places],
        scratch_shapes=scratch,
        compiler_params=pltpu.CompilerParams(vmem_limit_bytes=VMEM_LIMIT),
        cost_estimate=pl.CostEstimate(flops=flops, bytes_accessed=2**20, transcendentals=0),
    )(*inputs)


def exchange(array, axes):
    return lax.all_to_all(array, axes, split_axis=0, concat_axis=0, tiled=True)


def local(state, gates, gate_qubits, swap_order):
    scalars, vectors = [pltpu.SMEM] * 2, pltpu.VMEM
    place = [pltpu.SMEM((16,), I32)]
    rows = state.reshape(2, ROWS, DIM).transpose(1, 0, 2).reshape(2 * ROWS, DIM)
    sent = call(
        first_kernel,
        (gate_qubits, swap_order, rows, gates),
        jax.ShapeDtypeStruct((2 * ROWS, DIM), F32),
        [*scalars, vectors, vectors],
        place,
        3 * 10**9,
    )
    count = lax.axis_size(ALL)
    arrived = exchange(sent.reshape(count, -1, DIM), ALL).reshape(2 * ROWS, DIM)
    matrix = jax.ShapeDtypeStruct((4 * ROWS, ROWS), BF16)
    second, third = call(
        compose_kernel,
        (gate_qubits, swap_order, gates),
        [matrix, matrix],
        [*scalars, vectors],
        place,
        10**10,
    )
    narrow, tall = lax.axis_size("narrow"), lax.axis_size(Z)
    blocks, extremes = call(
        middle_kernel,
        (arrived, second, third),
        [
            jax.ShapeDtypeStruct((narrow, 2, DIM, DIM), F32),
            jax.ShapeDtypeStruct((tall, DIM), F32),
        ],
        [vectors] * 3,
        (),
        2 * 10**9,
    )
    extremes = exchange(extremes.reshape(tall, 1, DIM), Z)
    others = lax.axis_size(XCY)
    extremes = jnp.broadcast_to(jnp.max(extremes, axis=0, keepdims=True), (others, 1, DIM))
    extremes = exchange(extremes, XCY).reshape(others, DIM)
    returned = exchange(blocks, "narrow")
    out = call(
        last_kernel,
        (extremes, returned),
        jax.ShapeDtypeStruct((2 * ROWS, DIM), F32),
        [vectors] * 2,
        (),
        10**7,
    )
    return out.reshape(ROWS, 2, DIM).transpose(1, 0, 2).reshape(2, -1)


def solution(mesh):
    split = Mesh(mesh.devices.reshape(16, 4, 2, mesh.shape["narrow"]), ALL)
    return jax.shard_map(
        local,
        mesh=split,
        in_specs=(P(None, ALL), P(), P(), P()),
        out_specs=P(None, ALL),
        check_vma=False,
    )
```

time: 205 us -> 115 us (0.56)
  other arithmetic: 60.6 us -> 0.03 us
  local copies, waits for them, and re-layouts: 47.1 us -> 9.45 us
  Pallas kernels: 0 us -> 20.2 us
  blocking collectives: 55.3 us -> 36.4 us
  waiting for transfers between devices: 7.98 us -> 23.7 us
  matrix products: 4.9 us -> 0 us
  between operations: 3.67 us -> 0.07 us
    pmax x4 -> x0, blocking collectives: 55.3 us -> none  [over_axes(): shard = lax.pmax(shard, axis)]
    all_to_all x0 -> x3, blocking collectives: none -> 36.4 us  [exchange(): return lax.all_to_all(array, axes, split_axis=0, concat_axis=0, tiled=True)]
    gather x22 -> x0, local copies, waits for them, and re-layouts: 30 us -> none  [the longest x11 22.8 us: relayout(): jnp.take(rows_view, shuffle_index(layout, target, upper_count), axis=1)]
    sort x21 -> x0, other arithmetic: 27.4 us -> none  [the longest x11 14.4 us: shuffle_index(): position = jnp.argsort(source)]
    pallas_call x0 -> x4, Pallas kernels: none -> 20.2 us  [call(): pl.pallas_call(kernel, out_shape=outs, in_specs=[pl.BlockSpec(memory_spac...]
    select_n x34 -> x0, other arithmetic: 19.8 us -> none  [the longest x21 19.1 us: relayout(): jnp.take(rows_view, shuffle_index(layout, target, upper_count), axis=1)]
    all_to_all x2 -> x1, waiting for transfers between devices: 7.98 us -> 23.7 us  [exchange(): return lax.all_to_all(array, axes, split_axis=0, concat_axis=0, tiled=True)]
    scatter x10 -> x0, local copies, waits for them, and re-layouts: 5.93 us -> none  [top_order(): ranking.at[chosen]]
  transfers between devices with their start and end apart: 2 -> 1, of which waited for: 1 -> 1; matrix products, arithmetic and copies ran while one was open for 14% -> 0% of each run, Pallas kernels for 0% -> 9%
where the time goes in v1:
time: 115 us; the launch traced here: 114 us
  blocking collectives  36.4 us (32%)
  starting transfers between devices  24.3 us (21%)
  waiting for transfers between devices  23.7 us (21%)
  Pallas kernels  20.2 us (18%)
  local copies, waits for them, and re-layouts  9.45 us (8%)
    all_to_all x3, blocking collectives, exchange(): return lax.all_to_all(array, axes, split_axis=0, concat_axis=0, tiled=True)  36.4 us
    all_to_all x1, starting transfers between devices, exchange(): return lax.all_to_all(array, axes, split_axis=0, concat_axis=0, tiled=True)  24.3 us
    all_to_all x1, waiting for transfers between devices, exchange(): return lax.all_to_all(array, axes, split_axis=0, concat_axis=0, tiled=True)  23.7 us
    pallas_call x4, Pallas kernels, call(): pl.pallas_call(kernel, out_shape=outs, in_specs=[pl.BlockSpec(memory_spac...  20.2 us
    unnamed x22, local copies, waits for them, and re-layouts  9.43 us
  transfers between devices with their start and end apart: 1, of which 1 were waited for; matrix products, arithmetic and copies ran while one was open for 0% of the time, Pallas kernels for 9%

profile of v1, /device:TPU:1, one launch (start us, length us, event | category | flops | bytes accessed | tf_op | source)
XLA Modules:
  0.0 114.2 jit_solution(3855499425434067098)
XLA Ops:
  0.0 0.0 copy-start
  0.0 1.2 %copy-done = f32[8,2,128,128]{3,2,1,0:T(8,128)S(1)} copy-done((f32[8,2,128,128]{3,2,1,0:T(8,128)S(1)}, f32[8,2,128,128]{3,2,1,0:T(8,128)}, u32[]{:S(2)}) %copy-start) | copy-done | bytes 1048600
  1.2 0.0 copy-start.2
  1.2 1.0 copy-done.2
  2.3 0.0 copy-start.3
  2.3 0.7 copy-done.3
  3.0 0.0 copy-start.5
  3.0 0.7 copy-done.5
  3.6 0.0 copy-start.1
  3.6 0.0 copy-start.4
  3.6 0.0 copy-start.6
  3.6 4.7 %shard_map.46 = f32[1024,128]{1,0:T(8,128)} custom-call(s32[8,7]{1,0:T(8,128)S(1)} %copy-done.3, s32[9]{0:T(128)S(1)} %copy-done.5, f32[1024,128]{1,0:T(8,128)S(1)} %bitcast.19, f32[8,2,128,128]{3,2,1,0:T(8,128)S(1)} %copy-done), custom_call_target="tpu_custom_call" | custom-call | flops 3000000000 | bytes 1048576 | tf_op jit(solution)/shard_map/pallas_call | solution.py:192
  8.3 24.3 %all-to-all-start = ((f32[512,2,128]{2,1,0:T(2,128)}), f32[512,2,128]{2,1,0:T(2,128)S(1)}, u32[]{:S(2)}, u32[]{:S(2)}) async-start(f32[512,2,128]{2,1,0:T(2,128)} %bitcast.3), calls=%async_computation | async-start | bytes 1048576 | tf_op jit(solution)/shard_map/all_to_all | solution.py:203
  32.7 0.0 copy-done.1
  32.7 0.0 copy-done.4
  32.7 0.0 copy-done.6
  32.7 9.8 %shard_map.47 = (bf16[2048,512]{1,0:T(8,128)(2,1)S(1)}, bf16[2048,512]{1,0:T(8,128)(2,1)S(1)}) custom-call(s32[8,7]{1,0:T(8,128)S(1)} %copy-done.4, s32[9]{0:T(128)S(1)} %copy-done.6, f32[8,2,128,128]{3,2,1,0:T(8,128)S(1)} %copy-done.1), custom_call_target="tpu_custom_call" | custom-call | flops 10000000000 | bytes 1048576 | tf_op jit(solution)/shard_map/pallas_call | solution.py:192
  42.5 0.0 copy-start.7
  42.5 1.3 %copy-done.7 = bf16[2048,512]{1,0:T(8,128)(2,1)} copy-done((bf16[2048,512]{1,0:T(8,128)(2,1)}, bf16[2048,512]{1,0:T(8,128)(2,1)S(1)}, u32[]{:S(2)}) %copy-start.7) | copy-done | bytes 2097176
  43.9 0.0 copy-start.9
  43.9 1.3 %copy-done.9 = bf16[2048,512]{1,0:T(8,128)(2,1)} copy-done((bf16[2048,512]{1,0:T(8,128)(2,1)}, bf16[2048,512]{1,0:T(8,128)(2,1)S(1)}, u32[]{:S(2)}) %copy-start.9) | copy-done | bytes 2097176
  45.2 23.7 %all-to-all-done = f32[512,2,128]{2,1,0:T(2,128)S(1)} async-done(((f32[512,2,128]{2,1,0:T(2,128)}), f32[512,2,128]{2,1,0:T(2,128)S(1)}, u32[]{:S(2)}, u32[]{:S(2)}) %all-to-all-start) | async-done | bytes 524320 | tf_op jit(solution)/shard_map/all_to_all | solution.py:203
  68.9 0.0 copy-start.8
  68.9 1.6 %copy-done.8 = bf16[2048,512]{1,0:T(8,128)(2,1)S(1)} copy-done((bf16[2048,512]{1,0:T(8,128)(2,1)S(1)}, bf16[2048,512]{1,0:T(8,128)(2,1)}, u32[]{:S(2)}) %copy-start.8) | copy-done | bytes 2097176
  70.4 0.0 copy-start.10
  70.5 1.6 %copy-done.10 = bf16[2048,512]{1,0:T(8,128)(2,1)S(1)} copy-done((bf16[2048,512]{1,0:T(8,128)(2,1)S(1)}, bf16[2048,512]{1,0:T(8,128)(2,1)}, u32[]{:S(2)}) %copy-start.10) | copy-done | bytes 2097176
  72.0 4.1 %shard_map.48 = (f32[4,2,128,128]{3,2,1,0:T(8,128)S(1)}, f32[16,128]{1,0:T(8,128)S(1)}) custom-call(f32[1024,128]{1,0:T(8,128)S(1)} %bitcast.16, bf16[2048,512]{1,0:T(8,128)(2,1)S(1)} %copy-done.8, bf16[2048,512]{1,0:T(8,128)(2,1)S(1)} %copy-done.10), custom_call_target="tpu_custom_call" | custom-call | flops 2000000000 | bytes 1048576 | tf_op jit(solution)/shard_map/pallas_call | solution.py:192
  76.1 13.8 %all_to_all.20 = f32[16,1,128]{2,1,0:T(1,128)S(1)} all-to-all(f32[16,1,128]{2,1,0:T(1,128)S(1)} %bitcast.18), channel_id=1, replica_groups=mesh['z'=16,'x'=4,'core'=2,'narrow'=4] {'z'}, dimensions={0} | all-to-all | bytes 16384 | tf_op jit(solution)/shard_map/all_to_all | solution.py:203
  90.0 11.5 %all_to_all.21 = f32[32,1,128]{2,1,0:T(1,128)S(1)} all-to-all(f32[32,1,128]{2,1,0:T(1,128)S(1)} %broadcast_in_dim.2), channel_id=1, replica_groups=mesh['z'=16,'x'=4,'core'=2,'narrow'=4] {'x','core','narrow'}, dimensions={0} | all-to-all | bytes 32768 | tf_op jit(solution)/shard_map/all_to_all | solution.py:203
  101.5 11.0 %all_to_all.22.arrived_ref = f32[4,2,128,128]{3,2,1,0:T(8,128)S(1)} all-to-all(f32[4,2,128,128]{3,2,1,0:T(8,128)S(1)} %get-tuple-element.12), channel_id=1, replica_groups=mesh['z'=16,'x'=4,'core'=2,'narrow'=4] {'narrow'}, dimensions={0} | all-to-all | bytes 1048576 | tf_op jit(solution)/shard_map/all_to_all | solution.py:203
  112.5 1.6 %shard_map.49 = f32[1024,128]{1,0:T(8,128)} custom-call(f32[32,128]{1,0:T(8,128)S(1)} %bitcast.17, f32[4,2,128,128]{3,2,1,0:T(8,128)S(1)} %all_to_all.22.arrived_ref), custom_call_target="tpu_custom_call" | custom-call | flops 10000000 | bytes 1048576 | tf_op jit(solution)/shard_map/pallas_call | solution.py:192
  (2 shorter events, 0.0 us)
Async XLA Ops:
  0.0 1.2 %copy-start = (f32[8,2,128,128]{3,2,1,0:T(8,128)S(1)}, f32[8,2,128,128]{3,2,1,0:T(8,128)}, u32[]{:S(2)}) copy-start(f32[8,2,128,128]{3,2,1,0:T(8,128)} %gates_ref.3) | copy-start | bytes 3145732
  1.2 1.0 copy-start.2
  2.3 0.7 copy-start.3
  3.0 0.7 copy-start.5
  3.6 29.1 %copy-start.1 = (f32[8,2,128,128]{3,2,1,0:T(8,128)S(1)}, f32[8,2,128,128]{3,2,1,0:T(8,128)}, u32[]{:S(2)}) copy-start(f32[8,2,128,128]{3,2,1,0:T(8,128)} %gates_ref.3) | copy-start | bytes 3145732
  3.6 29.1 %copy-start.4 = (s32[8,7]{1,0:T(8,128)S(1)}, s32[8,7]{1,0:T(8,128)}, u32[]{:S(2)}) copy-start(s32[8,7]{1,0:T(8,128)} %gate_qubits.3) | copy-start | bytes 676
  3.6 29.1 %copy-start.6 = (s32[9]{0:T(128)S(1)}, s32[9]{0:T(128)}, u32[]{:S(2)}) copy-start(s32[9]{0:T(128)} %swap_order.3) | copy-start | bytes 112
  8.3 60.5 %all-to-all-start = ((f32[512,2,128]{2,1,0:T(2,128)}), f32[512,2,128]{2,1,0:T(2,128)S(1)}, u32[]{:S(2)}, u32[]{:S(2)}) async-start(f32[512,2,128]{2,1,0:T(2,128)} %bitcast.3), calls=%async_computation | async-start | bytes 1048576 | tf_op jit(solution)/shard_map/all_to_all | solution.py:203
  42.5 1.3 %copy-start.7 = (bf16[2048,512]{1,0:T(8,128)(2,1)}, bf16[2048,512]{1,0:T(8,128)(2,1)S(1)}, u32[]{:S(2)}) copy-start(bf16[2048,512]{1,0:T(8,128)(2,1)S(1)} %get-tuple-element.9.second_ref) | copy-start | bytes 6291460
  43.9 1.3 %copy-start.9 = (bf16[2048,512]{1,0:T(8,128)(2,1)}, bf16[2048,512]{1,0:T(8,128)(2,1)S(1)}, u32[]{:S(2)}) copy-start(bf16[2048,512]{1,0:T(8,128)(2,1)S(1)} %get-tuple-element.10.third_ref) | copy-start | bytes 6291460
  68.9 1.6 %copy-start.8 = (bf16[2048,512]{1,0:T(8,128)(2,1)S(1)}, bf16[2048,512]{1,0:T(8,128)(2,1)}, u32[]{:S(2)}) copy-start(bf16[2048,512]{1,0:T(8,128)(2,1)} %copy-done.7) | copy-start | bytes 6291460
  70.4 1.6 %copy-start.10 = (bf16[2048,512]{1,0:T(8,128)(2,1)S(1)}, bf16[2048,512]{1,0:T(8,128)(2,1)}, u32[]{:S(2)}) copy-start(bf16[2048,512]{1,0:T(8,128)(2,1)} %copy-done.9) | copy-start | bytes 6291460

commit v2 on v1

--- a/solution.py
+++ b/solution.py
@@ -13,13 +13,17 @@
 UPPER = 9
 ROWS = 2**UPPER
 DIM = 128
-Z, XCY = "z", ("x", "core", "narrow")
+TAIL = 8
+OTHERS = ("x", "core", "z")
 ALL = ("z", "x", "core", "narrow")
+SENT = ("x", "core", "narrow", "z")
 
 F32, BF16, I32 = jnp.float32, jnp.bfloat16, jnp.int32
 companding = 16.0
 companding_norm = math.log(16.0 + math.sqrt(257.0))
 VMEM_LIMIT = 40 * 2**20
+MIDDLE_LIMIT = 58 * 2**20
+LARGE_LIMIT = 60 * 2**20
 
 
 def dot(a, b):
@@ -44,7 +48,7 @@
 
 def swap_layout(swap_order):
     order = [swap_order[k] - LANE_QUBITS for k in range(UPPER)]
-    return order[2:] + order[:2]
+    return order[5:] + order[2:5] + order[:2]
 
 
 def permutation(source, target, place):
@@ -72,17 +76,21 @@
 def apply_gate(matrix, high, low):
     width = high.shape[1] // 2
     size = 2 * DIM
-    done = []
-    for other in range(ROWS // DIM):
-        rows = slice(other * DIM, (other + 1) * DIM)
-        stacked = jnp.concatenate([high[rows, :width], high[rows, width:]], axis=0)
-        both = dot(matrix, stacked)
-        mixed = both[:size] + both[size:]
-        if low is not None:
-            rest = jnp.concatenate([low[rows, :width], low[rows, width:]], axis=0)
-            mixed = mixed + dot(matrix[:size], rest)
-        done.append(jnp.concatenate([mixed[:DIM], mixed[DIM:]], axis=1))
-    return jnp.concatenate(done, axis=0)
+
+    def stack(part):
+        blocks = [part[DIM * i : DIM * (i + 1)] for i in range(4)]
+        real = jnp.concatenate([block[:, :width] for block in blocks], axis=1)
+        imag = jnp.concatenate([block[:, width:] for block in blocks], axis=1)
+        return jnp.concatenate([real, imag], axis=0)
+
+    both = dot(matrix, stack(high))
+    mixed = both[:size] + both[size:]
+    if low is not None:
+        mixed = mixed + dot(matrix[:size], stack(low))
+    columns = [mixed[:, width * i : width * (i + 1)] for i in range(4)]
+    return jnp.concatenate(
+        [jnp.concatenate([c[:DIM], c[DIM:]], axis=1) for c in columns], axis=0
+    )
 
 
 def permute(matrix, high, low):
@@ -108,7 +116,15 @@
     return [x[DIM * i : DIM * (i + 1)] for i in range(4)]
 
 
-def first_kernel(gate_qubits, swap_order, state_ref, gates_ref, out_ref, place):
+def first_kernel(
+    gate_qubits, swap_order, state_hbm, gates_hbm, out_ref, state_ref, gates_ref, place, done
+):
+    state_copy = pltpu.make_async_copy(state_hbm, state_ref, done.at[0])
+    gates_copy = pltpu.make_async_copy(gates_hbm.at[pl.ds(0, 3)], gates_ref, done.at[1])
+    state_copy.start()
+    gates_copy.start()
+    state_copy.wait()
+    gates_copy.wait()
     planes = [state_ref[pl.ds(p, ROWS, stride=2), :] for p in range(2)]
     high, low = pieces(jnp.concatenate(planes, axis=1))
     layout = None
@@ -121,12 +137,14 @@
     mixed = dot(matrix, high) + dot(matrix, low)
     for p in range(2):
         for y, slab in enumerate(quarters(slabs_of(mixed[:, DIM * p : DIM * (p + 1)]))):
-            out_ref[pl.ds(2 * y + p, DIM, stride=8), :] = slab
-
-
-def compose_kernel(gate_qubits, swap_order, gates_ref, second_ref, third_ref, place):
+            for block in range(8):
+                rows = slab[16 * block : 16 * (block + 1)]
+                out_ref[pl.ds(128 * block + 32 * y + p, 16, stride=2), :] = rows
+
+
+def compose_kernel(gate_qubits, swap_order, gates_ref, out_ref, place):
     swapped = swap_layout(swap_order)
-    for out_ref, numbers, last in ((second_ref, (3, 4, 5), swapped), (third_ref, (6, 7), None)):
+    for start, numbers, last in ((0, (3, 4, 5), swapped), (4 * ROWS, (6, 7), None)):
         layout = swapped
         for gate in numbers:
             target = gate_layout(gate_qubits, gate)
@@ -140,7 +158,7 @@
             high, low = pieces(apply_gate(gate_matrix(gates_ref, gate), high, low))
         high, low = permute(permutation(layout, last, place), high, low)
         for number, part in enumerate((high[:, :ROWS], high[:, ROWS:], low[:, :ROWS], low[:, ROWS:])):
-            out_ref[ROWS * number : ROWS * (number + 1), :] = part
+            out_ref[start + ROWS * number : start + ROWS * (number + 1), :] = part
 
 
 def apply_matrix(matrix_ref, real, imag):
@@ -153,23 +171,44 @@
     )
 
 
-def middle_kernel(arrived_ref, second_ref, third_ref, out_ref, extremes_ref):
-    planes = [
-        jnp.concatenate(
-            quarters([arrived_ref[pl.ds(2 * n + p, DIM, stride=8), :] for n in range(4)]), axis=0
-        )
-        for p in range(2)
-    ]
+def middle_kernel(
+    arrived_ref, matrices_hbm, out_ref, second_ref, third_ref, done
+):
+    second_copy = pltpu.make_async_copy(
+        matrices_hbm.at[pl.ds(0, 4 * ROWS)], second_ref, done.at[0])
+    third_copy = pltpu.make_async_copy(
+        matrices_hbm.at[pl.ds(4 * ROWS, 4 * ROWS)], third_ref, done.at[1])
+    second_copy.start()
+    third_copy.start()
+    planes = []
+    for p in range(2):
+        slabs = []
+        for n in range(4):
+            starts = [128 * block + 32 * n + p for block in range(8)]
+            rows = [arrived_ref[pl.ds(start, 16, stride=2), :] for start in starts]
+            slabs.append(jnp.concatenate(rows, axis=0))
+        planes.append(jnp.concatenate(quarters(slabs), axis=0))
+    second_copy.wait()
     planes = apply_matrix(second_ref, *planes)
     planes = [jnp.concatenate(quarters(slabs_of(x)), axis=0) for x in planes]
+    third_copy.wait()
     planes = apply_matrix(third_ref, *planes)
     highest = jnp.max(jnp.maximum(planes[0], planes[1]))
     lowest = jnp.min(jnp.minimum(planes[0], planes[1]))
-    lane = lax.broadcasted_iota(I32, extremes_ref.shape, 1)
-    extremes_ref[...] = jnp.where(lane < 64, highest, -lowest)
+    lane = lax.broadcasted_iota(I32, (TAIL, DIM), 1)
+    extremes = jnp.where(lane < 64, highest, -lowest)
     for p in range(2):
         for t, slab in enumerate(quarters(slabs_of(planes[p]))):
-            out_ref[t, p] = slab
+            out_ref[t, DIM * p : DIM * (p + 1), :] = slab
+    for t in range(4):
+        out_ref[t, 2 * DIM : 2 * DIM + TAIL, :] = extremes
+
+
+def reduce_kernel(arrived_ref, out_ref):
+    found = jnp.max(
+        jnp.max(arrived_ref[:, 2 * DIM : 2 * DIM + TAIL, :], axis=0), axis=0, keepdims=True
+    )
+    out_ref[...] = jnp.broadcast_to(found, out_ref.shape)
 
 
 def last_kernel(extremes_ref, arrived_ref, out_ref):
@@ -181,20 +220,20 @@
     middle = (highest + lowest) * 0.5
     halfwidth = (highest - lowest) * 0.5 + 1e-06
     for p in range(2):
-        for q, slab in enumerate(quarters([arrived_ref[y, p] for y in range(4)])):
+        for q, slab in enumerate(quarters([arrived_ref[y, DIM * p : DIM * (p + 1), :] for y in range(4)])):
             value = companding * (slab - middle) / halfwidth
             size = jnp.abs(value)
             curve = jnp.log(size + jnp.sqrt(size * size + 1.0)) / companding_norm
             out_ref[pl.ds(2 * DIM * q + p, DIM, stride=2), :] = jnp.where(value < 0, -curve, curve)
 
 
-def call(kernel, inputs, outs, places, scratch=(), flops=0, gates=False):
+def call(kernel, inputs, outs, places, scratch=(), flops=0, limit=VMEM_LIMIT):
     return pl.pallas_call(
         kernel,
         out_shape=outs,
         in_specs=[pl.BlockSpec(memory_space=m) for m in places],
         scratch_shapes=scratch,
-        compiler_params=pltpu.CompilerParams(vmem_limit_bytes=VMEM_LIMIT),
+        compiler_params=pltpu.CompilerParams(vmem_limit_bytes=limit),
         cost_estimate=pl.CostEstimate(flops=flops, bytes_accessed=2**20, transcendentals=0),
     )(*inputs)
 
@@ -204,45 +243,51 @@
 
 
 def local(state, gates, gate_qubits, swap_order):
-    scalars, vectors = [pltpu.SMEM] * 2, pltpu.VMEM
-    place = [pltpu.SMEM((16,), I32)]
+    scalars, vectors, remote = [pltpu.SMEM] * 2, pltpu.VMEM, pl.ANY
+    place, done = pltpu.SMEM((16,), I32), pltpu.SemaphoreType.DMA((2,))
     rows = state.reshape(2, ROWS, DIM).transpose(1, 0, 2).reshape(2 * ROWS, DIM)
     sent = call(
         first_kernel,
         (gate_qubits, swap_order, rows, gates),
         jax.ShapeDtypeStruct((2 * ROWS, DIM), F32),
-        [*scalars, vectors, vectors],
-        place,
+        [*scalars, remote, remote],
+        [
+            pltpu.VMEM((2 * ROWS, DIM), F32),
+            pltpu.VMEM((3, 2, DIM, DIM), F32),
+            place,
+            done,
+        ],
         3 * 10**9,
-    )
-    count = lax.axis_size(ALL)
-    arrived = exchange(sent.reshape(count, -1, DIM), ALL).reshape(2 * ROWS, DIM)
-    matrix = jax.ShapeDtypeStruct((4 * ROWS, ROWS), BF16)
-    second, third = call(
+        LARGE_LIMIT,
+    )
+    count = lax.axis_size(SENT)
+    arrived = exchange(sent.reshape(count, -1, DIM), SENT).reshape(2 * ROWS, DIM)
+    matrices = call(
         compose_kernel,
         (gate_qubits, swap_order, gates),
-        [matrix, matrix],
+        jax.ShapeDtypeStruct((8 * ROWS, ROWS), BF16),
         [*scalars, vectors],
-        place,
+        [place],
         10**10,
     )
-    narrow, tall = lax.axis_size("narrow"), lax.axis_size(Z)
-    blocks, extremes = call(
+    narrow, others = lax.axis_size("narrow"), lax.axis_size(OTHERS)
+    blocks = call(
         middle_kernel,
-        (arrived, second, third),
-        [
-            jax.ShapeDtypeStruct((narrow, 2, DIM, DIM), F32),
-            jax.ShapeDtypeStruct((tall, DIM), F32),
-        ],
-        [vectors] * 3,
-        (),
+        (arrived, matrices),
+        jax.ShapeDtypeStruct((narrow, 2 * DIM + TAIL, DIM), F32),
+        [vectors, pltpu.HBM],
+        [pltpu.VMEM((4 * ROWS, ROWS), BF16)] * 2 + [done],
         2 * 10**9,
-    )
-    extremes = exchange(extremes.reshape(tall, 1, DIM), Z)
-    others = lax.axis_size(XCY)
-    extremes = jnp.broadcast_to(jnp.max(extremes, axis=0, keepdims=True), (others, 1, DIM))
-    extremes = exchange(extremes, XCY).reshape(others, DIM)
+        MIDDLE_LIMIT,
+    )
     returned = exchange(blocks, "narrow")
+    extremes = call(
+        reduce_kernel,
+        (returned,),
+        jax.ShapeDtypeStruct((others, DIM), F32),
+        [vectors],
+    )
+    extremes = exchange(extremes.reshape(others, 1, DIM), OTHERS).reshape(others, DIM)
     out = call(
         last_kernel,
         (extremes, returned),

time: 115 us -> 111 us (0.965)
  local copies, waits for them, and re-layouts: 9.45 us -> 2.74 us
  Pallas kernels: 20.2 us -> 24.9 us
    unnamed x22 -> x10, local copies, waits for them, and re-layouts: 9.43 us -> 2.74 us
    pallas_call x4 -> x5, Pallas kernels: 20.2 us -> 24.9 us  [call(): pl.pallas_call(kernel, out_shape=outs, in_specs=[pl.BlockSpec(memory_spac...]
    all_to_all x3 -> x2, blocking collectives: 36.4 us -> 35.4 us  [exchange(): return lax.all_to_all(array, axes, split_axis=0, concat_axis=0, tiled=True)]
where the time goes in v2:
time: 111 us; the launch traced here: 110 us
  blocking collectives  35.4 us (32%)
  Pallas kernels  24.9 us (22%)
  starting transfers between devices  24.3 us (22%)
  waiting for transfers between devices  23.1 us (21%)
  local copies, waits for them, and re-layouts  2.74 us (2%)
    all_to_all x2, blocking collectives, exchange(): return lax.all_to_all(array, axes, split_axis=0, concat_axis=0, tiled=True)  35.4 us
    pallas_call x5, Pallas kernels, call(): pl.pallas_call(kernel, out_shape=outs, in_specs=[pl.BlockSpec(memory_spac...  24.9 us
    all_to_all x1, starting transfers between devices, exchange(): return lax.all_to_all(array, axes, split_axis=0, concat_axis=0, tiled=True)  24.3 us
    all_to_all x1, waiting for transfers between devices, exchange(): return lax.all_to_all(array, axes, split_axis=0, concat_axis=0, tiled=True)  23.1 us
    unnamed x10, local copies, waits for them, and re-layouts  2.74 us
  transfers between devices with their start and end apart: 1, of which 1 were waited for; matrix products, arithmetic and copies ran while one was open for 0% of the time, Pallas kernels for 9%

profile of v2, /device:TPU:1, one launch (start us, length us, event | category | flops | bytes accessed | tf_op | source)
XLA Modules:
  0.0 110.5 jit_solution(16809444039670338590)
XLA Ops:
  0.0 0.0 copy-start
  0.0 0.0 copy-start.1
  0.0 0.0 copy-start.2
  0.0 6.0 %shard_map.46 = f32[1024,128]{1,0:T(8,128)} custom-call(s32[8,7]{1,0:T(8,128)} %gate_qubits.3, s32[9]{0:T(128)} %swap_order.3, f32[1024,128]{1,0:T(8,128)} %bitcast.20, f32[8,2,128,128]{3,2,1,0:T(8,128)} %gates_ref.1), custom_call_target="tpu_custom_call" | custom-call | flops 3000000000 | bytes 1048576 | tf_op jit(solution)/shard_map/pallas_call | solution.py:231
  6.0 24.3 %all-to-all-start = ((f32[512,2,128]{2,1,0:T(2,128)}), f32[512,2,128]{2,1,0:T(2,128)S(1)}, u32[]{:S(2)}, u32[]{:S(2)}) async-start(f32[512,2,128]{2,1,0:T(2,128)} %bitcast.19), calls=%async_computation | async-start | bytes 1048576 | tf_op jit(solution)/shard_map/all_to_all | solution.py:242
  30.3 0.0 copy-done
  30.3 0.0 copy-done.1
  30.3 0.0 copy-done.2
  30.3 9.8 %shard_map.47.matrices_hbm = bf16[4096,512]{1,0:T(8,128)(2,1)S(1)} custom-call(s32[8,7]{1,0:T(8,128)S(1)} %copy-done.1, s32[9]{0:T(128)S(1)} %copy-done.2, f32[8,2,128,128]{3,2,1,0:T(8,128)S(1)} %copy-done), custom_call_target="tpu_custom_call" | custom-call | flops 10000000000 | bytes 1048576 | tf_op jit(solution)/shard_map/pallas_call | solution.py:231
  40.2 0.0 copy-start.3
  40.2 1.9 %copy-done.3 = bf16[4096,512]{1,0:T(8,128)(2,1)} copy-done((bf16[4096,512]{1,0:T(8,128)(2,1)}, bf16[4096,512]{1,0:T(8,128)(2,1)S(1)}, u32[]{:S(2)}) %copy-start.3) | copy-done | bytes 4194328
  42.1 23.1 %all-to-all-done = f32[512,2,128]{2,1,0:T(2,128)S(1)} async-done(((f32[512,2,128]{2,1,0:T(2,128)}), f32[512,2,128]{2,1,0:T(2,128)S(1)}, u32[]{:S(2)}, u32[]{:S(2)}) %all-to-all-start) | async-done | bytes 524320 | tf_op jit(solution)/shard_map/all_to_all | solution.py:242
  65.2 0.0 copy-start.4
  65.2 0.8 copy-done.4
  66.0 7.4 %shard_map.48 = f32[4,264,128]{2,1,0:T(8,128)} custom-call(f32[1024,128]{1,0:T(8,128)} %bitcast.18, bf16[4096,512]{1,0:T(8,128)(2,1)} %copy-done.3), custom_call_target="tpu_custom_call" | custom-call | flops 2000000000 | bytes 1048576 | tf_op jit(solution)/shard_map/pallas_call | solution.py:231
  73.4 11.4 %all_to_all.15.arrived_ref = f32[4,264,128]{2,1,0:T(8,128)S(1)} all-to-all(f32[4,264,128]{2,1,0:T(8,128)} %shard_map.48), channel_id=1, replica_groups=mesh['z'=16,'x'=4,'core'=2,'narrow'=4] {'narrow'}, dimensions={0} | all-to-all | bytes 1081344 | tf_op jit(solution)/shard_map/all_to_all | solution.py:242
  84.8 24.0 %all_to_all.16 = f32[128,1,128]{2,1,0:T(1,128)S(1)} all-to-all(f32[128,1,128]{2,1,0:T(1,128)S(1)} %bitcast.17), channel_id=1, replica_groups=mesh['z'=16,'x'=4,'core'=2,'narrow'=4] {'x','core','z'}, dimensions={0} | all-to-all | bytes 131072 | tf_op jit(solution)/shard_map/all_to_all | solution.py:242
  108.8 1.6 %shard_map.50 = f32[1024,128]{1,0:T(8,128)} custom-call(f32[128,128]{1,0:T(8,128)S(1)} %bitcast.16, f32[4,264,128]{2,1,0:T(8,128)S(1)} %all_to_all.15.arrived_ref), custom_call_target="tpu_custom_call" | custom-call | flops 10000000 | bytes 1048576 | tf_op jit(solution)/shard_map/pallas_call | solution.py:231
  (1 shorter events, 0.0 us)
Async XLA Ops:
  0.0 30.3 %copy-start = (f32[8,2,128,128]{3,2,1,0:T(8,128)S(1)}, f32[8,2,128,128]{3,2,1,0:T(8,128)}, u32[]{:S(2)}) copy-start(f32[8,2,128,128]{3,2,1,0:T(8,128)} %gates_ref.1) | copy-start | bytes 3145732
  0.0 30.3 %copy-start.1 = (s32[8,7]{1,0:T(8,128)S(1)}, s32[8,7]{1,0:T(8,128)}, u32[]{:S(2)}) copy-start(s32[8,7]{1,0:T(8,128)} %gate_qubits.3) | copy-start | bytes 676
  0.0 30.3 %copy-start.2 = (s32[9]{0:T(128)S(1)}, s32[9]{0:T(128)}, u32[]{:S(2)}) copy-start(s32[9]{0:T(128)} %swap_order.3) | copy-start | bytes 112
  6.0 59.2 %all-to-all-start = ((f32[512,2,128]{2,1,0:T(2,128)}), f32[512,2,128]{2,1,0:T(2,128)S(1)}, u32[]{:S(2)}, u32[]{:S(2)}) async-start(f32[512,2,128]{2,1,0:T(2,128)} %bitcast.19), calls=%async_computation | async-start | bytes 1048576 | tf_op jit(solution)/shard_map/all_to_all | solution.py:242
  40.2 1.9 %copy-start.3 = (bf16[4096,512]{1,0:T(8,128)(2,1)}, bf16[4096,512]{1,0:T(8,128)(2,1)S(1)}, u32[]{:S(2)}) copy-start(bf16[4096,512]{1,0:T(8,128)(2,1)S(1)} %shard_map.47.matrices_hbm) | copy-start | bytes 12582916
  65.2 0.8 copy-start.4

commit v3 on v2

--- a/solution.py
+++ b/solution.py
@@ -13,8 +13,9 @@
 UPPER = 9
 ROWS = 2**UPPER
 DIM = 128
+PART = 32
 TAIL = 8
-OTHERS = ("x", "core", "z")
+LAST, OTHERS = ("x", "narrow"), ("core", "z")
 ALL = ("z", "x", "core", "narrow")
 SENT = ("x", "core", "narrow", "z")
 
@@ -22,7 +23,7 @@
 companding = 16.0
 companding_norm = math.log(16.0 + math.sqrt(257.0))
 VMEM_LIMIT = 40 * 2**20
-MIDDLE_LIMIT = 58 * 2**20
+MIDDLE_LIMIT = 52 * 2**20
 LARGE_LIMIT = 60 * 2**20
 
 
@@ -69,24 +70,27 @@
     real, imag = gates_ref[gate, 0], gates_ref[gate, 1]
     top = jnp.concatenate([real, -imag], axis=1)
     bottom = jnp.concatenate([imag, real], axis=1)
-    high, low = pieces(jnp.concatenate([top, bottom], axis=0))
-    return jnp.concatenate([high, low], axis=0)
+    return pieces(jnp.concatenate([top, bottom], axis=0))
 
 
 def apply_gate(matrix, high, low):
     width = high.shape[1] // 2
-    size = 2 * DIM
 
     def stack(part):
-        blocks = [part[DIM * i : DIM * (i + 1)] for i in range(4)]
+        blocks = slabs_of(part)
         real = jnp.concatenate([block[:, :width] for block in blocks], axis=1)
         imag = jnp.concatenate([block[:, width:] for block in blocks], axis=1)
         return jnp.concatenate([real, imag], axis=0)
 
-    both = dot(matrix, stack(high))
-    mixed = both[:size] + both[size:]
-    if low is not None:
-        mixed = mixed + dot(matrix[:size], stack(low))
+    upper, lower = matrix
+    if low is None:
+        left = jnp.concatenate([upper, lower], axis=1)
+        right = jnp.concatenate([stack(high)] * 2, axis=0)
+    else:
+        stacked = stack(high)
+        left = jnp.concatenate([upper, upper, lower], axis=1)
+        right = jnp.concatenate([stacked, stack(low), stacked], axis=0)
+    mixed = dot(left, right)
     columns = [mixed[:, width * i : width * (i + 1)] for i in range(4)]
     return jnp.concatenate(
         [jnp.concatenate([c[:DIM], c[DIM:]], axis=1) for c in columns], axis=0
@@ -97,23 +101,32 @@
     return dot(matrix, high).astype(BF16), dot(matrix, low).astype(BF16)
 
 
+def slabs_of(x, count=4):
+    size = x.shape[0] // count
+    return [x[size * i : size * (i + 1)] for i in range(count)]
+
+
+def exchange_bit(slabs, bit, width):
+    lane = lax.broadcasted_iota(I32, slabs[0].shape, 1)
+    clear = (lane & width) == 0
+    out = list(slabs)
+    for i in range(len(slabs)):
+        j = i | bit
+        if i != j:
+            out[i] = jnp.where(clear, slabs[i], pltpu.roll(slabs[j], width, 1))
+            out[j] = jnp.where(clear, pltpu.roll(slabs[i], DIM - width, 1), slabs[j])
+    return out
+
+
 def quarters(slabs):
-    lane = lax.broadcasted_iota(I32, slabs[0].shape, 1)
-    first = lane < 64
-    half = [None] * 4
-    for i in range(2):
-        half[i] = jnp.where(first, slabs[i], pltpu.roll(slabs[i + 2], 64, 1))
-        half[i + 2] = jnp.where(first, pltpu.roll(slabs[i], 64, 1), slabs[i + 2])
-    even = (lane & 32) == 0
-    out = [None] * 4
-    for i in (0, 2):
-        out[i] = jnp.where(even, half[i], pltpu.roll(half[i + 1], 32, 1))
-        out[i + 1] = jnp.where(even, pltpu.roll(half[i], 96, 1), half[i + 1])
-    return out
-
-
-def slabs_of(x):
-    return [x[DIM * i : DIM * (i + 1)] for i in range(4)]
+    return exchange_bit(exchange_bit(slabs, 1, 32), 2, 64)
+
+
+def sixteenths(x):
+    slabs = slabs_of(x, 16)
+    for k in range(4):
+        slabs = exchange_bit(slabs, 1 << k, 8 << k)
+    return slabs
 
 
 def first_kernel(
@@ -123,23 +136,26 @@
     gates_copy = pltpu.make_async_copy(gates_hbm.at[pl.ds(0, 3)], gates_ref, done.at[1])
     state_copy.start()
     gates_copy.start()
+    targets = [gate_layout(gate_qubits, gate) for gate in range(3)]
+    matrix = permutation(None, targets[0], place)
     state_copy.wait()
-    gates_copy.wait()
     planes = [state_ref[pl.ds(p, ROWS, stride=2), :] for p in range(2)]
     high, low = pieces(jnp.concatenate(planes, axis=1))
-    layout = None
+    high, low = permute(matrix, high, low)
+    gates_copy.wait()
     for gate in range(3):
-        target = gate_layout(gate_qubits, gate)
-        high, low = permute(permutation(layout, target, place), high, low)
-        layout = target
         high, low = pieces(apply_gate(gate_matrix(gates_ref, gate), high, low))
-    matrix = permutation(layout, swap_layout(swap_order), place)
+        target = targets[gate + 1] if gate < 2 else swap_layout(swap_order)
+        matrix = permutation(targets[gate], target, place)
+        if gate < 2:
+            high, low = permute(matrix, high, low)
     mixed = dot(matrix, high) + dot(matrix, low)
     for p in range(2):
-        for y, slab in enumerate(quarters(slabs_of(mixed[:, DIM * p : DIM * (p + 1)]))):
-            for block in range(8):
-                rows = slab[16 * block : 16 * (block + 1)]
-                out_ref[pl.ds(128 * block + 32 * y + p, 16, stride=2), :] = rows
+        for number, slab in enumerate(sixteenths(mixed[:, DIM * p : DIM * (p + 1)])):
+            x, y = number // 4, number % 4
+            for core in range(2):
+                start = 128 * (2 * x + core) + 32 * y + p
+                out_ref[pl.ds(start, 16, stride=2), :] = slab[16 * core : 16 * (core + 1)]
 
 
 def compose_kernel(gate_qubits, swap_order, gates_ref, out_ref, place):
@@ -161,25 +177,39 @@
             out_ref[start + ROWS * number : start + ROWS * (number + 1), :] = part
 
 
-def apply_matrix(matrix_ref, real, imag):
+def apply_matrix(matrix_ref, copies, real, imag):
     high, low = pieces(jnp.concatenate([real, imag], axis=1))
-    both = dot(matrix_ref[...], high)
-    total = both[: 2 * ROWS] + both[2 * ROWS :] + dot(matrix_ref[: 2 * ROWS, :], low)
+    total = []
+    right = jnp.concatenate([high, low], axis=0)
+    for number in range(2):
+        copies[number].wait()
+        part = matrix_ref[ROWS * number : ROWS * (number + 1), :]
+        total.append(dot(jnp.concatenate([part, part], axis=1), right))
+    for number in range(2):
+        copies[number + 2].wait()
+        total[number] = total[number] + dot(
+            matrix_ref[ROWS * (number + 2) : ROWS * (number + 3), :], high
+        )
     return (
-        total[:ROWS, :DIM] - total[ROWS:, DIM:],
-        total[ROWS:, :DIM] + total[:ROWS, DIM:],
+        total[0][:, :DIM] - total[1][:, DIM:],
+        total[1][:, :DIM] + total[0][:, DIM:],
     )
 
 
 def middle_kernel(
     arrived_ref, matrices_hbm, out_ref, second_ref, third_ref, done
 ):
-    second_copy = pltpu.make_async_copy(
-        matrices_hbm.at[pl.ds(0, 4 * ROWS)], second_ref, done.at[0])
-    third_copy = pltpu.make_async_copy(
-        matrices_hbm.at[pl.ds(4 * ROWS, 4 * ROWS)], third_ref, done.at[1])
-    second_copy.start()
-    third_copy.start()
+    copies = []
+    for number in range(8):
+        target = (second_ref, third_ref)[number // 4]
+        copies.append(
+            pltpu.make_async_copy(
+                matrices_hbm.at[pl.ds(ROWS * number, ROWS)],
+                target.at[pl.ds(ROWS * (number % 4), ROWS)],
+                done.at[number],
+            )
+        )
+        copies[number].start()
     planes = []
     for p in range(2):
         slabs = []
@@ -188,25 +218,24 @@
             rows = [arrived_ref[pl.ds(start, 16, stride=2), :] for start in starts]
             slabs.append(jnp.concatenate(rows, axis=0))
         planes.append(jnp.concatenate(quarters(slabs), axis=0))
-    second_copy.wait()
-    planes = apply_matrix(second_ref, *planes)
+    planes = apply_matrix(second_ref, copies[:4], *planes)
     planes = [jnp.concatenate(quarters(slabs_of(x)), axis=0) for x in planes]
-    third_copy.wait()
-    planes = apply_matrix(third_ref, *planes)
+    planes = apply_matrix(third_ref, copies[4:], *planes)
     highest = jnp.max(jnp.maximum(planes[0], planes[1]))
     lowest = jnp.min(jnp.minimum(planes[0], planes[1]))
     lane = lax.broadcasted_iota(I32, (TAIL, DIM), 1)
     extremes = jnp.where(lane < 64, highest, -lowest)
     for p in range(2):
-        for t, slab in enumerate(quarters(slabs_of(planes[p]))):
-            out_ref[t, DIM * p : DIM * (p + 1), :] = slab
-    for t in range(4):
-        out_ref[t, 2 * DIM : 2 * DIM + TAIL, :] = extremes
+        for number, slab in enumerate(sixteenths(planes[p])):
+            target = 4 * (number % 4) + number // 4
+            out_ref[target, PART * p : PART * (p + 1), :] = slab
+    for target in range(16):
+        out_ref[target, 2 * PART : 2 * PART + TAIL, :] = extremes
 
 
 def reduce_kernel(arrived_ref, out_ref):
     found = jnp.max(
-        jnp.max(arrived_ref[:, 2 * DIM : 2 * DIM + TAIL, :], axis=0), axis=0, keepdims=True
+        jnp.max(arrived_ref[:, 2 * PART : 2 * PART + TAIL, :], axis=0), axis=0, keepdims=True
     )
     out_ref[...] = jnp.broadcast_to(found, out_ref.shape)
 
@@ -220,11 +249,12 @@
     middle = (highest + lowest) * 0.5
     halfwidth = (highest - lowest) * 0.5 + 1e-06
     for p in range(2):
-        for q, slab in enumerate(quarters([arrived_ref[y, DIM * p : DIM * (p + 1), :] for y in range(4)])):
+        rows = [arrived_ref[n, PART * p : PART * (p + 1), :] for n in range(16)]
+        for q, slab in enumerate(sixteenths(jnp.concatenate(rows, axis=0))):
             value = companding * (slab - middle) / halfwidth
             size = jnp.abs(value)
             curve = jnp.log(size + jnp.sqrt(size * size + 1.0)) / companding_norm
-            out_ref[pl.ds(2 * DIM * q + p, DIM, stride=2), :] = jnp.where(value < 0, -curve, curve)
+            out_ref[pl.ds(2 * PART * q + p, PART, stride=2), :] = jnp.where(value < 0, -curve, curve)
 
 
 def call(kernel, inputs, outs, places, scratch=(), flops=0, limit=VMEM_LIMIT):
@@ -270,17 +300,17 @@
         [place],
         10**10,
     )
-    narrow, others = lax.axis_size("narrow"), lax.axis_size(OTHERS)
+    targets, others = lax.axis_size(LAST), lax.axis_size(OTHERS)
     blocks = call(
         middle_kernel,
         (arrived, matrices),
-        jax.ShapeDtypeStruct((narrow, 2 * DIM + TAIL, DIM), F32),
+        jax.ShapeDtypeStruct((targets, 2 * PART + TAIL, DIM), F32),
         [vectors, pltpu.HBM],
-        [pltpu.VMEM((4 * ROWS, ROWS), BF16)] * 2 + [done],
+        [pltpu.VMEM((4 * ROWS, ROWS), BF16)] * 2 + [pltpu.SemaphoreType.DMA((8,))],
         2 * 10**9,
         MIDDLE_LIMIT,
     )
-    returned = exchange(blocks, "narrow")
+    returned = exchange(blocks, LAST)
     extremes = call(
         reduce_kernel,
         (returned,),

time: 111 us -> 105 us (0.946)
  blocking collectives: 35.4 us -> 31.8 us
    all_to_all x2, blocking collectives: 35.4 us -> 31.8 us  [exchange(): return lax.all_to_all(array, axes, split_axis=0, concat_axis=0, tiled=True)]
    unnamed x10 -> x8, local copies, waits for them, and re-layouts: 2.74 us -> 1.94 us
where the time goes in v3:
time: 105 us
  blocking collectives  31.8 us (30%)
  starting transfers between devices  24.3 us (23%)
  Pallas kernels  24.2 us (23%)
  waiting for transfers between devices  22.9 us (22%)
  local copies, waits for them, and re-layouts  1.94 us (2%)
    all_to_all x2, blocking collectives, exchange(): return lax.all_to_all(array, axes, split_axis=0, concat_axis=0, tiled=True)  31.8 us
    all_to_all x1, starting transfers between devices, exchange(): return lax.all_to_all(array, axes, split_axis=0, concat_axis=0, tiled=True)  24.3 us
    pallas_call x5, Pallas kernels, call(): pl.pallas_call(kernel, out_shape=outs, in_specs=[pl.BlockSpec(memory_spac...  24.2 us
    all_to_all x1, waiting for transfers between devices, exchange(): return lax.all_to_all(array, axes, split_axis=0, concat_axis=0, tiled=True)  22.9 us
  transfers between devices with their start and end apart: 1, of which 1 were waited for; matrix products, arithmetic and copies ran while one was open for 0% of the time, Pallas kernels for 9%

profile of v3, /device:TPU:1, one launch (start us, length us, event | category | flops | bytes accessed | tf_op | source)
XLA Modules:
  0.0 105.2 jit_solution(11066240471454008819)
XLA Ops:
  0.0 0.0 copy-start
  0.0 0.0 copy-start.1
  0.0 0.0 copy-start.2
  0.0 6.3 %shard_map.46 = f32[1024,128]{1,0:T(8,128)} custom-call(s32[8,7]{1,0:T(8,128)} %gate_qubits.3, s32[9]{0:T(128)} %swap_order.3, f32[1024,128]{1,0:T(8,128)} %bitcast.20, f32[8,2,128,128]{3,2,1,0:T(8,128)} %gates_ref.1), custom_call_target="tpu_custom_call" | custom-call | flops 3000000000 | bytes 1048576 | tf_op jit(solution)/shard_map/pallas_call | solution.py:261
  6.3 24.3 %all-to-all-start = ((f32[512,2,128]{2,1,0:T(2,128)}), f32[512,2,128]{2,1,0:T(2,128)S(1)}, u32[]{:S(2)}, u32[]{:S(2)}) async-start(f32[512,2,128]{2,1,0:T(2,128)} %bitcast.19), calls=%async_computation | async-start | bytes 1048576 | tf_op jit(solution)/shard_map/all_to_all | solution.py:272
  30.7 0.0 copy-done
  30.7 0.0 copy-done.1
  30.7 0.0 copy-done.2
  30.7 10.0 %shard_map.47.matrices_hbm = bf16[4096,512]{1,0:T(8,128)(2,1)S(1)} custom-call(s32[8,7]{1,0:T(8,128)S(1)} %copy-done.1, s32[9]{0:T(128)S(1)} %copy-done.2, f32[8,2,128,128]{3,2,1,0:T(8,128)S(1)} %copy-done), custom_call_target="tpu_custom_call" | custom-call | flops 10000000000 | bytes 1048576 | tf_op jit(solution)/shard_map/pallas_call | solution.py:261
  40.7 0.0 copy-start.3
  40.7 1.9 %copy-done.3 = bf16[4096,512]{1,0:T(8,128)(2,1)} copy-done((bf16[4096,512]{1,0:T(8,128)(2,1)}, bf16[4096,512]{1,0:T(8,128)(2,1)S(1)}, u32[]{:S(2)}) %copy-start.3) | copy-done | bytes 4194328
  42.6 22.9 %all-to-all-done = f32[512,2,128]{2,1,0:T(2,128)S(1)} async-done(((f32[512,2,128]{2,1,0:T(2,128)}), f32[512,2,128]{2,1,0:T(2,128)S(1)}, u32[]{:S(2)}, u32[]{:S(2)}) %all-to-all-start) | async-done | bytes 524320 | tf_op jit(solution)/shard_map/all_to_all | solution.py:272
  65.5 6.1 %shard_map.48 = f32[16,72,128]{2,1,0:T(8,128)S(1)} custom-call(f32[1024,128]{1,0:T(8,128)S(1)} %bitcast.16, bf16[4096,512]{1,0:T(8,128)(2,1)} %copy-done.3), custom_call_target="tpu_custom_call" | custom-call | flops 2000000000 | bytes 1048576 | tf_op jit(solution)/shard_map/pallas_call | solution.py:261
  71.6 15.4 %all_to_all.15.arrived_ref = f32[16,72,128]{2,1,0:T(8,128)S(1)} all-to-all(f32[16,72,128]{2,1,0:T(8,128)S(1)} %shard_map.48), channel_id=1, replica_groups=mesh['z'=16,'x'=4,'core'=2,'narrow'=4] {'x','narrow'}, dimensions={0} | all-to-all | bytes 1179648 | tf_op jit(solution)/shard_map/all_to_all | solution.py:272
  87.0 16.4 %all_to_all.16 = f32[32,1,128]{2,1,0:T(1,128)S(1)} all-to-all(f32[32,1,128]{2,1,0:T(1,128)S(1)} %bitcast.18), channel_id=1, replica_groups=mesh['z'=16,'x'=4,'core'=2,'narrow'=4] {'core','z'}, dimensions={0} | all-to-all | bytes 32768 | tf_op jit(solution)/shard_map/all_to_all | solution.py:272
  103.4 1.8 %shard_map.50 = f32[1024,128]{1,0:T(8,128)} custom-call(f32[32,128]{1,0:T(8,128)S(1)} %bitcast.17, f32[16,72,128]{2,1,0:T(8,128)S(1)} %all_to_all.15.arrived_ref), custom_call_target="tpu_custom_call" | custom-call | flops 10000000 | bytes 1048576 | tf_op jit(solution)/shard_map/pallas_call | solution.py:261
  (1 shorter events, 0.0 us)
Async XLA Ops:
  0.0 30.7 %copy-start = (f32[8,2,128,128]{3,2,1,0:T(8,128)S(1)}, f32[8,2,128,128]{3,2,1,0:T(8,128)}, u32[]{:S(2)}) copy-start(f32[8,2,128,128]{3,2,1,0:T(8,128)} %gates_ref.1) | copy-start | bytes 3145732
  0.0 30.7 %copy-start.1 = (s32[8,7]{1,0:T(8,128)S(1)}, s32[8,7]{1,0:T(8,128)}, u32[]{:S(2)}) copy-start(s32[8,7]{1,0:T(8,128)} %gate_qubits.3) | copy-start | bytes 676
  0.0 30.7 %copy-start.2 = (s32[9]{0:T(128)S(1)}, s32[9]{0:T(128)}, u32[]{:S(2)}) copy-start(s32[9]{0:T(128)} %swap_order.3) | copy-start | bytes 112
  6.3 59.2 %all-to-all-start = ((f32[512,2,128]{2,1,0:T(2,128)}), f32[512,2,128]{2,1,0:T(2,128)S(1)}, u32[]{:S(2)}, u32[]{:S(2)}) async-start(f32[512,2,128]{2,1,0:T(2,128)} %bitcast.19), calls=%async_computation | async-start | bytes 1048576 | tf_op jit(solution)/shard_map/all_to_all | solution.py:272
  40.7 1.9 %copy-start.3 = (bf16[4096,512]{1,0:T(8,128)(2,1)}, bf16[4096,512]{1,0:T(8,128)(2,1)S(1)}, u32[]{:S(2)}) copy-start(bf16[4096,512]{1,0:T(8,128)(2,1)S(1)} %shard_map.47.matrices_hbm) | copy-start | bytes 12582916

commit v4 on v3

--- a/solution.py
+++ b/solution.py
@@ -18,6 +18,7 @@
 LAST, OTHERS = ("x", "narrow"), ("core", "z")
 ALL = ("z", "x", "core", "narrow")
 SENT = ("x", "core", "narrow", "z")
+STRIDES = {"x": 128, "core": 64, "narrow": 16, "z": 1}
 
 F32, BF16, I32 = jnp.float32, jnp.bfloat16, jnp.int32
 companding = 16.0
@@ -129,14 +130,36 @@
     return slabs
 
 
+def block_rows(x, core, narrow, plane):
+    start = sum(STRIDES[a] * i for a, i in (("x", x), ("core", core), ("narrow", narrow)))
+    return pl.ds(2 * start + plane, 16, stride=2 * STRIDES["z"])
+
+
 def first_kernel(
-    gate_qubits, swap_order, state_hbm, gates_hbm, out_ref, state_ref, gates_ref, place, done
+    qubits_hbm,
+    order_hbm,
+    state_hbm,
+    gates_hbm,
+    out_ref,
+    gate_qubits,
+    swap_order,
+    state_ref,
+    gates_ref,
+    place,
+    done,
 ):
+    qubits_copy = pltpu.make_async_copy(qubits_hbm, gate_qubits, done.at[2])
+    order_copy = pltpu.make_async_copy(order_hbm, swap_order, done.at[3])
+    qubits_copy.start()
+    order_copy.start()
     state_copy = pltpu.make_async_copy(state_hbm, state_ref, done.at[0])
     gates_copy = pltpu.make_async_copy(gates_hbm.at[pl.ds(0, 3)], gates_ref, done.at[1])
     state_copy.start()
     gates_copy.start()
+    qubits_copy.wait()
+    order_copy.wait()
     targets = [gate_layout(gate_qubits, gate) for gate in range(3)]
+    targets.append(swap_layout(swap_order))
     matrix = permutation(None, targets[0], place)
     state_copy.wait()
     planes = [state_ref[pl.ds(p, ROWS, stride=2), :] for p in range(2)]
@@ -145,8 +168,7 @@
     gates_copy.wait()
     for gate in range(3):
         high, low = pieces(apply_gate(gate_matrix(gates_ref, gate), high, low))
-        target = targets[gate + 1] if gate < 2 else swap_layout(swap_order)
-        matrix = permutation(targets[gate], target, place)
+        matrix = permutation(targets[gate], targets[gate + 1], place)
         if gate < 2:
             high, low = permute(matrix, high, low)
     mixed = dot(matrix, high) + dot(matrix, low)
@@ -154,8 +176,8 @@
         for number, slab in enumerate(sixteenths(mixed[:, DIM * p : DIM * (p + 1)])):
             x, y = number // 4, number % 4
             for core in range(2):
-                start = 128 * (2 * x + core) + 32 * y + p
-                out_ref[pl.ds(start, 16, stride=2), :] = slab[16 * core : 16 * (core + 1)]
+                rows = slab[16 * core : 16 * (core + 1)]
+                out_ref[block_rows(x, core, y, p), :] = rows
 
 
 def compose_kernel(gate_qubits, swap_order, gates_ref, out_ref, place):
@@ -177,19 +199,14 @@
             out_ref[start + ROWS * number : start + ROWS * (number + 1), :] = part
 
 
-def apply_matrix(matrix_ref, copies, real, imag):
+def apply_matrix(matrix_ref, real, imag):
     high, low = pieces(jnp.concatenate([real, imag], axis=1))
+    right = jnp.concatenate([high, low], axis=0)
     total = []
-    right = jnp.concatenate([high, low], axis=0)
     for number in range(2):
-        copies[number].wait()
-        part = matrix_ref[ROWS * number : ROWS * (number + 1), :]
-        total.append(dot(jnp.concatenate([part, part], axis=1), right))
-    for number in range(2):
-        copies[number + 2].wait()
-        total[number] = total[number] + dot(
-            matrix_ref[ROWS * (number + 2) : ROWS * (number + 3), :], high
-        )
+        upper = matrix_ref[ROWS * number : ROWS * (number + 1), :]
+        lower = matrix_ref[ROWS * (number + 2) : ROWS * (number + 3), :]
+        total.append(dot(jnp.concatenate([upper, upper], axis=1), right) + dot(lower, high))
     return (
         total[0][:, :DIM] - total[1][:, DIM:],
         total[1][:, :DIM] + total[0][:, DIM:],
@@ -199,28 +216,28 @@
 def middle_kernel(
     arrived_ref, matrices_hbm, out_ref, second_ref, third_ref, done
 ):
-    copies = []
-    for number in range(8):
-        target = (second_ref, third_ref)[number // 4]
-        copies.append(
-            pltpu.make_async_copy(
-                matrices_hbm.at[pl.ds(ROWS * number, ROWS)],
-                target.at[pl.ds(ROWS * (number % 4), ROWS)],
-                done.at[number],
-            )
+    copies = [
+        pltpu.make_async_copy(
+            matrices_hbm.at[pl.ds(4 * ROWS * number, 4 * ROWS)], target, done.at[number]
         )
-        copies[number].start()
+        for number, target in enumerate((second_ref, third_ref))
+    ]
+    for copy in copies:
+        copy.start()
     planes = []
     for p in range(2):
         slabs = []
         for n in range(4):
-            starts = [128 * block + 32 * n + p for block in range(8)]
-            rows = [arrived_ref[pl.ds(start, 16, stride=2), :] for start in starts]
+            rows = [
+                arrived_ref[block_rows(block // 2, block % 2, n, p), :] for block in range(8)
+            ]
             slabs.append(jnp.concatenate(rows, axis=0))
         planes.append(jnp.concatenate(quarters(slabs), axis=0))
-    planes = apply_matrix(second_ref, copies[:4], *planes)
+    copies[0].wait()
+    planes = apply_matrix(second_ref, *planes)
     planes = [jnp.concatenate(quarters(slabs_of(x)), axis=0) for x in planes]
-    planes = apply_matrix(third_ref, copies[4:], *planes)
+    copies[1].wait()
+    planes = apply_matrix(third_ref, *planes)
     highest = jnp.max(jnp.maximum(planes[0], planes[1]))
     lowest = jnp.min(jnp.minimum(planes[0], planes[1]))
     lane = lax.broadcasted_iota(I32, (TAIL, DIM), 1)
@@ -248,12 +265,14 @@
     lowest = -jnp.max(jnp.where(lane < 64, least, found))
     middle = (highest + lowest) * 0.5
     halfwidth = (highest - lowest) * 0.5 + 1e-06
+    scale = jnp.full((8, DIM), companding, F32) / halfwidth
+    scale = jnp.concatenate([scale] * (PART // 8), axis=0)
     for p in range(2):
         rows = [arrived_ref[n, PART * p : PART * (p + 1), :] for n in range(16)]
         for q, slab in enumerate(sixteenths(jnp.concatenate(rows, axis=0))):
-            value = companding * (slab - middle) / halfwidth
+            value = (slab - middle) * scale
             size = jnp.abs(value)
-            curve = jnp.log(size + jnp.sqrt(size * size + 1.0)) / companding_norm
+            curve = jnp.log(size + jnp.sqrt(size * size + 1.0)) * (1.0 / companding_norm)
             out_ref[pl.ds(2 * PART * q + p, PART, stride=2), :] = jnp.where(value < 0, -curve, curve)
 
 
@@ -274,14 +293,16 @@
 
 def local(state, gates, gate_qubits, swap_order):
     scalars, vectors, remote = [pltpu.SMEM] * 2, pltpu.VMEM, pl.ANY
-    place, done = pltpu.SMEM((16,), I32), pltpu.SemaphoreType.DMA((2,))
+    place, done = pltpu.SMEM((16,), I32), pltpu.SemaphoreType.DMA((4,))
     rows = state.reshape(2, ROWS, DIM).transpose(1, 0, 2).reshape(2 * ROWS, DIM)
     sent = call(
         first_kernel,
         (gate_qubits, swap_order, rows, gates),
         jax.ShapeDtypeStruct((2 * ROWS, DIM), F32),
-        [*scalars, remote, remote],
+        [remote] * 4,
         [
+            pltpu.SMEM(gate_qubits.shape, I32),
+            pltpu.SMEM(swap_order.shape, I32),
             pltpu.VMEM((2 * ROWS, DIM), F32),
             pltpu.VMEM((3, 2, DIM, DIM), F32),
             place,
@@ -306,7 +327,7 @@
         (arrived, matrices),
         jax.ShapeDtypeStruct((targets, 2 * PART + TAIL, DIM), F32),
         [vectors, pltpu.HBM],
-        [pltpu.VMEM((4 * ROWS, ROWS), BF16)] * 2 + [pltpu.SemaphoreType.DMA((8,))],
+        [pltpu.VMEM((4 * ROWS, ROWS), BF16)] * 2 + [pltpu.SemaphoreType.DMA((2,))],
         2 * 10**9,
         MIDDLE_LIMIT,
     )

time: 105 us -> 103 us (0.981)
  Pallas kernels: 24.2 us -> 21.9 us
    pallas_call x5, Pallas kernels: 24.2 us -> 21.9 us  [call(): pl.pallas_call(kernel, out_shape=outs, in_specs=[pl.BlockSpec(memory_spac...]
  transfers between devices with their start and end apart: 1 -> 1, of which waited for: 1 -> 1; matrix products, arithmetic and copies ran while one was open for 0% -> 0% of each run, Pallas kernels for 9% -> 10%
where the time goes in v4:
time: 103 us
  blocking collectives  31.8 us (31%)
  starting transfers between devices  24.3 us (24%)
  waiting for transfers between devices  22.9 us (22%)
  Pallas kernels  21.9 us (21%)
  local copies, waits for them, and re-layouts  1.94 us (2%)
    all_to_all x2, blocking collectives, exchange(): return lax.all_to_all(array, axes, split_axis=0, concat_axis=0, tiled=True)  31.8 us
    all_to_all x1, starting transfers between devices, exchange(): return lax.all_to_all(array, axes, split_axis=0, concat_axis=0, tiled=True)  24.3 us
    all_to_all x1, waiting for transfers between devices, exchange(): return lax.all_to_all(array, axes, split_axis=0, concat_axis=0, tiled=True)  22.9 us
    pallas_call x5, Pallas kernels, call(): pl.pallas_call(kernel, out_shape=outs, in_specs=[pl.BlockSpec(memory_spac...  21.9 us
  transfers between devices with their start and end apart: 1, of which 1 were waited for; matrix products, arithmetic and copies ran while one was open for 0% of the time, Pallas kernels for 10%

profile of v4, /device:TPU:1, one launch (start us, length us, event | category | flops | bytes accessed | tf_op | source)
XLA Modules:
  0.0 102.9 jit_solution(5126675807687202180)
XLA Ops:
  0.0 0.0 copy-start
  0.0 0.0 copy-start.1
  0.0 0.0 copy-start.2
  0.0 5.6 %shard_map.46 = f32[1024,128]{1,0:T(8,128)} custom-call(s32[8,7]{1,0:T(8,128)} %gate_qubits.1, s32[9]{0:T(128)} %swap_order.1, f32[1024,128]{1,0:T(8,128)} %bitcast.20, f32[8,2,128,128]{3,2,1,0:T(8,128)} %gates_ref.1), custom_call_target="tpu_custom_call" | custom-call | flops 3000000000 | bytes 1048576 | tf_op jit(solution)/shard_map/pallas_call | solution.py:280
  5.6 24.3 %all-to-all-start = ((f32[512,2,128]{2,1,0:T(2,128)}), f32[512,2,128]{2,1,0:T(2,128)S(1)}, u32[]{:S(2)}, u32[]{:S(2)}) async-start(f32[512,2,128]{2,1,0:T(2,128)} %bitcast.19), calls=%async_computation | async-start | bytes 1048576 | tf_op jit(solution)/shard_map/all_to_all | solution.py:291
  29.9 0.0 copy-done
  29.9 0.0 copy-done.1
  29.9 0.0 copy-done.2
  29.9 10.0 %shard_map.47.matrices_hbm = bf16[4096,512]{1,0:T(8,128)(2,1)S(1)} custom-call(s32[8,7]{1,0:T(8,128)S(1)} %copy-done.1, s32[9]{0:T(128)S(1)} %copy-done.2, f32[8,2,128,128]{3,2,1,0:T(8,128)S(1)} %copy-done), custom_call_target="tpu_custom_call" | custom-call | flops 10000000000 | bytes 1048576 | tf_op jit(solution)/shard_map/pallas_call | solution.py:280
  39.9 0.0 copy-start.3
  39.9 1.9 %copy-done.3 = bf16[4096,512]{1,0:T(8,128)(2,1)} copy-done((bf16[4096,512]{1,0:T(8,128)(2,1)}, bf16[4096,512]{1,0:T(8,128)(2,1)S(1)}, u32[]{:S(2)}) %copy-start.3) | copy-done | bytes 4194328
  41.9 22.9 %all-to-all-done = f32[512,2,128]{2,1,0:T(2,128)S(1)} async-done(((f32[512,2,128]{2,1,0:T(2,128)}), f32[512,2,128]{2,1,0:T(2,128)S(1)}, u32[]{:S(2)}, u32[]{:S(2)}) %all-to-all-start) | async-done | bytes 524320 | tf_op jit(solution)/shard_map/all_to_all | solution.py:291
  64.8 4.5 %shard_map.48 = f32[16,72,128]{2,1,0:T(8,128)S(1)} custom-call(f32[1024,128]{1,0:T(8,128)S(1)} %bitcast.16, bf16[4096,512]{1,0:T(8,128)(2,1)} %copy-done.3), custom_call_target="tpu_custom_call" | custom-call | flops 2000000000 | bytes 1048576 | tf_op jit(solution)/shard_map/pallas_call | solution.py:280
  69.3 15.4 %all_to_all.15.arrived_ref = f32[16,72,128]{2,1,0:T(8,128)S(1)} all-to-all(f32[16,72,128]{2,1,0:T(8,128)S(1)} %shard_map.48), channel_id=1, replica_groups=mesh['z'=16,'x'=4,'core'=2,'narrow'=4] {'x','narrow'}, dimensions={0} | all-to-all | bytes 1179648 | tf_op jit(solution)/shard_map/all_to_all | solution.py:291
  84.7 16.4 %all_to_all.16 = f32[32,1,128]{2,1,0:T(1,128)S(1)} all-to-all(f32[32,1,128]{2,1,0:T(1,128)S(1)} %bitcast.18), channel_id=1, replica_groups=mesh['z'=16,'x'=4,'core'=2,'narrow'=4] {'core','z'}, dimensions={0} | all-to-all | bytes 32768 | tf_op jit(solution)/shard_map/all_to_all | solution.py:291
  101.1 1.8 %shard_map.50 = f32[1024,128]{1,0:T(8,128)} custom-call(f32[32,128]{1,0:T(8,128)S(1)} %bitcast.17, f32[16,72,128]{2,1,0:T(8,128)S(1)} %all_to_all.15.arrived_ref), custom_call_target="tpu_custom_call" | custom-call | flops 10000000 | bytes 1048576 | tf_op jit(solution)/shard_map/pallas_call | solution.py:280
  (1 shorter events, 0.0 us)
Async XLA Ops:
  0.0 29.9 %copy-start = (f32[8,2,128,128]{3,2,1,0:T(8,128)S(1)}, f32[8,2,128,128]{3,2,1,0:T(8,128)}, u32[]{:S(2)}) copy-start(f32[8,2,128,128]{3,2,1,0:T(8,128)} %gates_ref.1) | copy-start | bytes 3145732
  0.0 29.9 %copy-start.1 = (s32[8,7]{1,0:T(8,128)S(1)}, s32[8,7]{1,0:T(8,128)}, u32[]{:S(2)}) copy-start(s32[8,7]{1,0:T(8,128)} %gate_qubits.1) | copy-start | bytes 676
  0.0 29.9 %copy-start.2 = (s32[9]{0:T(128)S(1)}, s32[9]{0:T(128)}, u32[]{:S(2)}) copy-start(s32[9]{0:T(128)} %swap_order.1) | copy-start | bytes 112
  5.6 59.2 %all-to-all-start = ((f32[512,2,128]{2,1,0:T(2,128)}), f32[512,2,128]{2,1,0:T(2,128)S(1)}, u32[]{:S(2)}, u32[]{:S(2)}) async-start(f32[512,2,128]{2,1,0:T(2,128)} %bitcast.19), calls=%async_computation | async-start | bytes 1048576 | tf_op jit(solution)/shard_map/all_to_all | solution.py:291
  39.9 1.9 %copy-start.3 = (bf16[4096,512]{1,0:T(8,128)(2,1)}, bf16[4096,512]{1,0:T(8,128)(2,1)S(1)}, u32[]{:S(2)}) copy-start(bf16[4096,512]{1,0:T(8,128)(2,1)S(1)} %shard_map.47.matrices_hbm) | copy-start | bytes 12582916

commit v5 on v4

--- a/solution.py
+++ b/solution.py
@@ -107,27 +107,30 @@
     return [x[size * i : size * (i + 1)] for i in range(count)]
 
 
-def exchange_bit(slabs, bit, width):
+def exchanged(slabs):
+    count = len(slabs)
+    width = DIM // count
     lane = lax.broadcasted_iota(I32, slabs[0].shape, 1)
-    clear = (lane & width) == 0
-    out = list(slabs)
-    for i in range(len(slabs)):
-        j = i | bit
-        if i != j:
-            out[i] = jnp.where(clear, slabs[i], pltpu.roll(slabs[j], width, 1))
-            out[j] = jnp.where(clear, pltpu.roll(slabs[i], DIM - width, 1), slabs[j])
-    return out
+    turned = [pltpu.roll(x, width * i, 1) if i else x for i, x in enumerate(slabs)]
+    step = 1
+    while step < count:
+        moves = (lane & (width * step)) != 0
+        turned = [
+            jnp.where(moves, turned[(i + step) % count], turned[i]) for i in range(count)
+        ]
+        step *= 2
+    return [
+        pltpu.roll(turned[-i % count], DIM - width * i, 1) if i else turned[0]
+        for i in range(count)
+    ]
 
 
 def quarters(slabs):
-    return exchange_bit(exchange_bit(slabs, 1, 32), 2, 64)
+    return exchanged(slabs)
 
 
 def sixteenths(x):
-    slabs = slabs_of(x, 16)
-    for k in range(4):
-        slabs = exchange_bit(slabs, 1 << k, 8 << k)
-    return slabs
+    return exchanged(slabs_of(x, 16))
 
 
 def block_rows(x, core, narrow, plane):

time: 103 us -> 103 us (level)
  no operation moved by 1% of the time
where the time goes in v5:
time: 103 us; the launch traced here: 102 us
  blocking collectives  31.8 us (31%)
  starting transfers between devices  24.3 us (24%)
  waiting for transfers between devices  22.9 us (22%)
  Pallas kernels  21.3 us (21%)
  local copies, waits for them, and re-layouts  1.94 us (2%)
    all_to_all x2, blocking collectives, exchange(): return lax.all_to_all(array, axes, split_axis=0, concat_axis=0, tiled=True)  31.8 us
    all_to_all x1, starting transfers between devices, exchange(): return lax.all_to_all(array, axes, split_axis=0, concat_axis=0, tiled=True)  24.3 us
    all_to_all x1, waiting for transfers between devices, exchange(): return lax.all_to_all(array, axes, split_axis=0, concat_axis=0, tiled=True)  22.9 us
    pallas_call x5, Pallas kernels, call(): pl.pallas_call(kernel, out_shape=outs, in_specs=[pl.BlockSpec(memory_spac...  21.3 us
  transfers between devices with their start and end apart: 1, of which 1 were waited for; matrix products, arithmetic and copies ran while one was open for 0% of the time, Pallas kernels for 10%

profile of v5, /device:TPU:1, one launch (start us, length us, event | category | flops | bytes accessed | tf_op | source)
XLA Modules:
  0.0 102.4 jit_solution(16859750584932691209)
XLA Ops:
  0.0 0.0 copy-start
  0.0 0.0 copy-start.1
  0.0 0.0 copy-start.2
  0.0 5.4 %shard_map.46 = f32[1024,128]{1,0:T(8,128)} custom-call(s32[8,7]{1,0:T(8,128)} %gate_qubits.1, s32[9]{0:T(128)} %swap_order.1, f32[1024,128]{1,0:T(8,128)} %bitcast.20, f32[8,2,128,128]{3,2,1,0:T(8,128)} %gates_ref.1), custom_call_target="tpu_custom_call" | custom-call | flops 3000000000 | bytes 1048576 | tf_op jit(solution)/shard_map/pallas_call | solution.py:283
  5.4 24.3 %all-to-all-start = ((f32[512,2,128]{2,1,0:T(2,128)}), f32[512,2,128]{2,1,0:T(2,128)S(1)}, u32[]{:S(2)}, u32[]{:S(2)}) async-start(f32[512,2,128]{2,1,0:T(2,128)} %bitcast.19), calls=%async_computation | async-start | bytes 1048576 | tf_op jit(solution)/shard_map/all_to_all | solution.py:294
  29.7 0.0 copy-done
  29.7 0.0 copy-done.1
  29.7 0.0 copy-done.2
  29.7 10.0 %shard_map.47.matrices_hbm = bf16[4096,512]{1,0:T(8,128)(2,1)S(1)} custom-call(s32[8,7]{1,0:T(8,128)S(1)} %copy-done.1, s32[9]{0:T(128)S(1)} %copy-done.2, f32[8,2,128,128]{3,2,1,0:T(8,128)S(1)} %copy-done), custom_call_target="tpu_custom_call" | custom-call | flops 10000000000 | bytes 1048576 | tf_op jit(solution)/shard_map/pallas_call | solution.py:283
  39.7 0.0 copy-start.3
  39.7 1.9 %copy-done.3 = bf16[4096,512]{1,0:T(8,128)(2,1)} copy-done((bf16[4096,512]{1,0:T(8,128)(2,1)}, bf16[4096,512]{1,0:T(8,128)(2,1)S(1)}, u32[]{:S(2)}) %copy-start.3) | copy-done | bytes 4194328
  41.7 22.9 %all-to-all-done = f32[512,2,128]{2,1,0:T(2,128)S(1)} async-done(((f32[512,2,128]{2,1,0:T(2,128)}), f32[512,2,128]{2,1,0:T(2,128)S(1)}, u32[]{:S(2)}, u32[]{:S(2)}) %all-to-all-start) | async-done | bytes 524320 | tf_op jit(solution)/shard_map/all_to_all | solution.py:294
  64.6 4.3 %shard_map.48 = f32[16,72,128]{2,1,0:T(8,128)S(1)} custom-call(f32[1024,128]{1,0:T(8,128)S(1)} %bitcast.16, bf16[4096,512]{1,0:T(8,128)(2,1)} %copy-done.3), custom_call_target="tpu_custom_call" | custom-call | flops 2000000000 | bytes 1048576 | tf_op jit(solution)/shard_map/pallas_call | solution.py:283
  68.9 15.4 %all_to_all.15.arrived_ref = f32[16,72,128]{2,1,0:T(8,128)S(1)} all-to-all(f32[16,72,128]{2,1,0:T(8,128)S(1)} %shard_map.48), channel_id=1, replica_groups=mesh['z'=16,'x'=4,'core'=2,'narrow'=4] {'x','narrow'}, dimensions={0} | all-to-all | bytes 1179648 | tf_op jit(solution)/shard_map/all_to_all | solution.py:294
  84.3 16.4 %all_to_all.16 = f32[32,1,128]{2,1,0:T(1,128)S(1)} all-to-all(f32[32,1,128]{2,1,0:T(1,128)S(1)} %bitcast.18), channel_id=1, replica_groups=mesh['z'=16,'x'=4,'core'=2,'narrow'=4] {'core','z'}, dimensions={0} | all-to-all | bytes 32768 | tf_op jit(solution)/shard_map/all_to_all | solution.py:294
  100.7 1.7 %shard_map.50 = f32[1024,128]{1,0:T(8,128)} custom-call(f32[32,128]{1,0:T(8,128)S(1)} %bitcast.17, f32[16,72,128]{2,1,0:T(8,128)S(1)} %all_to_all.15.arrived_ref), custom_call_target="tpu_custom_call" | custom-call | flops 10000000 | bytes 1048576 | tf_op jit(solution)/shard_map/pallas_call | solution.py:283
  (1 shorter events, 0.0 us)
Async XLA Ops:
  0.0 29.7 %copy-start = (f32[8,2,128,128]{3,2,1,0:T(8,128)S(1)}, f32[8,2,128,128]{3,2,1,0:T(8,128)}, u32[]{:S(2)}) copy-start(f32[8,2,128,128]{3,2,1,0:T(8,128)} %gates_ref.1) | copy-start | bytes 3145732
  0.0 29.7 %copy-start.1 = (s32[8,7]{1,0:T(8,128)S(1)}, s32[8,7]{1,0:T(8,128)}, u32[]{:S(2)}) copy-start(s32[8,7]{1,0:T(8,128)} %gate_qubits.1) | copy-start | bytes 676
  0.0 29.7 %copy-start.2 = (s32[9]{0:T(128)S(1)}, s32[9]{0:T(128)}, u32[]{:S(2)}) copy-start(s32[9]{0:T(128)} %swap_order.1) | copy-start | bytes 112
  5.4 59.2 %all-to-all-start = ((f32[512,2,128]{2,1,0:T(2,128)}), f32[512,2,128]{2,1,0:T(2,128)S(1)}, u32[]{:S(2)}, u32[]{:S(2)}) async-start(f32[512,2,128]{2,1,0:T(2,128)} %bitcast.19), calls=%async_computation | async-start | bytes 1048576 | tf_op jit(solution)/shard_map/all_to_all | solution.py:294
  39.7 1.9 %copy-start.3 = (bf16[4096,512]{1,0:T(8,128)(2,1)}, bf16[4096,512]{1,0:T(8,128)(2,1)S(1)}, u32[]{:S(2)}) copy-start(bf16[4096,512]{1,0:T(8,128)(2,1)S(1)} %shard_map.47.matrices_hbm) | copy-start | bytes 12582916

commit v6 on v5

--- a/solution.py
+++ b/solution.py
@@ -99,7 +99,11 @@
 
 
 def permute(matrix, high, low):
-    return dot(matrix, high).astype(BF16), dot(matrix, low).astype(BF16)
+    blocks = [matrix[:256], matrix[256:]]
+    return tuple(
+        jnp.concatenate([dot(block, part).astype(BF16) for block in blocks], axis=0)
+        for part in (high, low)
+    )
 
 
 def slabs_of(x, count=4):

time: 103 us -> 102 us (level)
  no operation moved by 1% of the time
where the time goes in v6:
time: 102 us
  blocking collectives  31.8 us (31%)
  starting transfers between devices  24.3 us (24%)
  waiting for transfers between devices  22.8 us (22%)
  Pallas kernels  21 us (21%)
  local copies, waits for them, and re-layouts  1.94 us (2%)
    all_to_all x2, blocking collectives, exchange(): return lax.all_to_all(array, axes, split_axis=0, concat_axis=0, tiled=True)  31.8 us
    all_to_all x1, starting transfers between devices, exchange(): return lax.all_to_all(array, axes, split_axis=0, concat_axis=0, tiled=True)  24.3 us
    all_to_all x1, waiting for transfers between devices, exchange(): return lax.all_to_all(array, axes, split_axis=0, concat_axis=0, tiled=True)  22.8 us
    pallas_call x5, Pallas kernels, call(): pl.pallas_call(kernel, out_shape=outs, in_specs=[pl.BlockSpec(memory_spac...  21 us
  transfers between devices with their start and end apart: 1, of which 1 were waited for; matrix products, arithmetic and copies ran while one was open for 0% of the time, Pallas kernels for 10%

profile of v6, /device:TPU:1, one launch (start us, length us, event | category | flops | bytes accessed | tf_op | source)
XLA Modules:
  0.0 101.9 jit_solution(18398006417804887150)
XLA Ops:
  0.0 0.0 copy-start
  0.0 0.0 copy-start.1
  0.0 0.0 copy-start.2
  0.0 4.9 %shard_map.46 = f32[1024,128]{1,0:T(8,128)} custom-call(s32[8,7]{1,0:T(8,128)} %gate_qubits.1, s32[9]{0:T(128)} %swap_order.1, f32[1024,128]{1,0:T(8,128)} %bitcast.20, f32[8,2,128,128]{3,2,1,0:T(8,128)} %gates_ref.1), custom_call_target="tpu_custom_call" | custom-call | flops 3000000000 | bytes 1048576 | tf_op jit(solution)/shard_map/pallas_call | solution.py:287
  4.9 24.3 %all-to-all-start = ((f32[512,2,128]{2,1,0:T(2,128)}), f32[512,2,128]{2,1,0:T(2,128)S(1)}, u32[]{:S(2)}, u32[]{:S(2)}) async-start(f32[512,2,128]{2,1,0:T(2,128)} %bitcast.19), calls=%async_computation | async-start | bytes 1048576 | tf_op jit(solution)/shard_map/all_to_all | solution.py:298
  29.3 0.0 copy-done
  29.3 0.0 copy-done.1
  29.3 0.0 copy-done.2
  29.3 10.1 %shard_map.47.matrices_hbm = bf16[4096,512]{1,0:T(8,128)(2,1)S(1)} custom-call(s32[8,7]{1,0:T(8,128)S(1)} %copy-done.1, s32[9]{0:T(128)S(1)} %copy-done.2, f32[8,2,128,128]{3,2,1,0:T(8,128)S(1)} %copy-done), custom_call_target="tpu_custom_call" | custom-call | flops 10000000000 | bytes 1048576 | tf_op jit(solution)/shard_map/pallas_call | solution.py:287
  39.4 0.0 copy-start.3
  39.4 1.9 %copy-done.3 = bf16[4096,512]{1,0:T(8,128)(2,1)} copy-done((bf16[4096,512]{1,0:T(8,128)(2,1)}, bf16[4096,512]{1,0:T(8,128)(2,1)S(1)}, u32[]{:S(2)}) %copy-start.3) | copy-done | bytes 4194328
  41.4 22.8 %all-to-all-done = f32[512,2,128]{2,1,0:T(2,128)S(1)} async-done(((f32[512,2,128]{2,1,0:T(2,128)}), f32[512,2,128]{2,1,0:T(2,128)S(1)}, u32[]{:S(2)}, u32[]{:S(2)}) %all-to-all-start) | async-done | bytes 524320 | tf_op jit(solution)/shard_map/all_to_all | solution.py:298
  64.1 4.3 %shard_map.48 = f32[16,72,128]{2,1,0:T(8,128)S(1)} custom-call(f32[1024,128]{1,0:T(8,128)S(1)} %bitcast.16, bf16[4096,512]{1,0:T(8,128)(2,1)} %copy-done.3), custom_call_target="tpu_custom_call" | custom-call | flops 2000000000 | bytes 1048576 | tf_op jit(solution)/shard_map/pallas_call | solution.py:287
  68.4 15.4 %all_to_all.15.arrived_ref = f32[16,72,128]{2,1,0:T(8,128)S(1)} all-to-all(f32[16,72,128]{2,1,0:T(8,128)S(1)} %shard_map.48), channel_id=1, replica_groups=mesh['z'=16,'x'=4,'core'=2,'narrow'=4] {'x','narrow'}, dimensions={0} | all-to-all | bytes 1179648 | tf_op jit(solution)/shard_map/all_to_all | solution.py:298
  83.9 16.4 %all_to_all.16 = f32[32,1,128]{2,1,0:T(1,128)S(1)} all-to-all(f32[32,1,128]{2,1,0:T(1,128)S(1)} %bitcast.18), channel_id=1, replica_groups=mesh['z'=16,'x'=4,'core'=2,'narrow'=4] {'core','z'}, dimensions={0} | all-to-all | bytes 32768 | tf_op jit(solution)/shard_map/all_to_all | solution.py:298
  100.3 1.7 %shard_map.50 = f32[1024,128]{1,0:T(8,128)} custom-call(f32[32,128]{1,0:T(8,128)S(1)} %bitcast.17, f32[16,72,128]{2,1,0:T(8,128)S(1)} %all_to_all.15.arrived_ref), custom_call_target="tpu_custom_call" | custom-call | flops 10000000 | bytes 1048576 | tf_op jit(solution)/shard_map/pallas_call | solution.py:287
  (1 shorter events, 0.0 us)
Async XLA Ops:
  0.0 29.3 %copy-start = (f32[8,2,128,128]{3,2,1,0:T(8,128)S(1)}, f32[8,2,128,128]{3,2,1,0:T(8,128)}, u32[]{:S(2)}) copy-start(f32[8,2,128,128]{3,2,1,0:T(8,128)} %gates_ref.1) | copy-start | bytes 3145732
  0.0 29.3 %copy-start.1 = (s32[8,7]{1,0:T(8,128)S(1)}, s32[8,7]{1,0:T(8,128)}, u32[]{:S(2)}) copy-start(s32[8,7]{1,0:T(8,128)} %gate_qubits.1) | copy-start | bytes 676
  0.0 29.3 %copy-start.2 = (s32[9]{0:T(128)S(1)}, s32[9]{0:T(128)}, u32[]{:S(2)}) copy-start(s32[9]{0:T(128)} %swap_order.1) | copy-start | bytes 112
  4.9 59.2 %all-to-all-start = ((f32[512,2,128]{2,1,0:T(2,128)}), f32[512,2,128]{2,1,0:T(2,128)S(1)}, u32[]{:S(2)}, u32[]{:S(2)}) async-start(f32[512,2,128]{2,1,0:T(2,128)} %bitcast.19), calls=%async_computation | async-start | bytes 1048576 | tf_op jit(solution)/shard_map/all_to_all | solution.py:298
  39.4 1.9 %copy-start.3 = (bf16[4096,512]{1,0:T(8,128)(2,1)}, bf16[4096,512]{1,0:T(8,128)(2,1)S(1)}, u32[]{:S(2)}) copy-start(bf16[4096,512]{1,0:T(8,128)(2,1)S(1)} %shard_map.47.matrices_hbm) | copy-start | bytes 12582916

commit v7 on v6

--- a/solution.py
+++ b/solution.py
@@ -202,18 +202,23 @@
             layout = target
             high, low = pieces(apply_gate(gate_matrix(gates_ref, gate), high, low))
         high, low = permute(permutation(layout, last, place), high, low)
-        for number, part in enumerate((high[:, :ROWS], high[:, ROWS:], low[:, :ROWS], low[:, ROWS:])):
+        for number, part in enumerate((high[:, :ROWS], low[:, :ROWS], high[:, ROWS:], low[:, ROWS:])):
             out_ref[start + ROWS * number : start + ROWS * (number + 1), :] = part
 
 
-def apply_matrix(matrix_ref, real, imag):
+def apply_matrix(matrix_ref, copies, real, imag):
     high, low = pieces(jnp.concatenate([real, imag], axis=1))
-    right = jnp.concatenate([high, low], axis=0)
+    right = jnp.concatenate([high, low, high], axis=0)
     total = []
     for number in range(2):
-        upper = matrix_ref[ROWS * number : ROWS * (number + 1), :]
-        lower = matrix_ref[ROWS * (number + 2) : ROWS * (number + 3), :]
-        total.append(dot(jnp.concatenate([upper, upper], axis=1), right) + dot(lower, high))
+        if number < len(copies):
+            copies[number].wait()
+        rows = []
+        for start in range(2 * ROWS * number, 2 * ROWS * number + ROWS, 128):
+            upper = matrix_ref[start : start + 128, :]
+            lower = matrix_ref[start + ROWS : start + ROWS + 128, :]
+            rows.append(dot(jnp.concatenate([upper, upper, lower], axis=1), right))
+        total.append(jnp.concatenate(rows, axis=0))
     return (
         total[0][:, :DIM] - total[1][:, DIM:],
         total[1][:, :DIM] + total[0][:, DIM:],
@@ -225,9 +230,15 @@
 ):
     copies = [
         pltpu.make_async_copy(
-            matrices_hbm.at[pl.ds(4 * ROWS * number, 4 * ROWS)], target, done.at[number]
+            matrices_hbm.at[pl.ds(start, size)], target, done.at[number]
         )
-        for number, target in enumerate((second_ref, third_ref))
+        for number, (start, size, target) in enumerate(
+            (
+                (0, 2 * ROWS, second_ref.at[pl.ds(0, 2 * ROWS)]),
+                (2 * ROWS, 2 * ROWS, second_ref.at[pl.ds(2 * ROWS, 2 * ROWS)]),
+                (4 * ROWS, 4 * ROWS, third_ref),
+            )
+        )
     ]
     for copy in copies:
         copy.start()
@@ -240,11 +251,9 @@
             ]
             slabs.append(jnp.concatenate(rows, axis=0))
         planes.append(jnp.concatenate(quarters(slabs), axis=0))
-    copies[0].wait()
-    planes = apply_matrix(second_ref, *planes)
+    planes = apply_matrix(second_ref, copies[:2], *planes)
     planes = [jnp.concatenate(quarters(slabs_of(x)), axis=0) for x in planes]
-    copies[1].wait()
-    planes = apply_matrix(third_ref, *planes)
+    planes = apply_matrix(third_ref, copies[2:], *planes)
     highest = jnp.max(jnp.maximum(planes[0], planes[1]))
     lowest = jnp.min(jnp.minimum(planes[0], planes[1]))
     lane = lax.broadcasted_iota(I32, (TAIL, DIM), 1)
@@ -334,7 +343,7 @@
         (arrived, matrices),
         jax.ShapeDtypeStruct((targets, 2 * PART + TAIL, DIM), F32),
         [vectors, pltpu.HBM],
-        [pltpu.VMEM((4 * ROWS, ROWS), BF16)] * 2 + [pltpu.SemaphoreType.DMA((2,))],
+        [pltpu.VMEM((4 * ROWS, ROWS), BF16)] * 2 + [pltpu.SemaphoreType.DMA((3,))],
         2 * 10**9,
         MIDDLE_LIMIT,
     )

time: 102 us -> 102 us (level)
  no operation moved by 1% of the time
where the time goes in v7:
time: 102 us
  blocking collectives  31.8 us (31%)
  starting transfers between devices  24.3 us (24%)
  waiting for transfers between devices  22.8 us (22%)
  Pallas kernels  20.9 us (20%)
  local copies, waits for them, and re-layouts  1.94 us (2%)
    all_to_all x2, blocking collectives, exchange(): return lax.all_to_all(array, axes, split_axis=0, concat_axis=0, tiled=True)  31.8 us
    all_to_all x1, starting transfers between devices, exchange(): return lax.all_to_all(array, axes, split_axis=0, concat_axis=0, tiled=True)  24.3 us
    all_to_all x1, waiting for transfers between devices, exchange(): return lax.all_to_all(array, axes, split_axis=0, concat_axis=0, tiled=True)  22.8 us
    pallas_call x5, Pallas kernels, call(): pl.pallas_call(kernel, out_shape=outs, in_specs=[pl.BlockSpec(memory_spac...  20.9 us
  transfers between devices with their start and end apart: 1, of which 1 were waited for; matrix products, arithmetic and copies ran while one was open for 0% of the time, Pallas kernels for 10%

profile of v7, /device:TPU:1, one launch (start us, length us, event | category | flops | bytes accessed | tf_op | source)
XLA Modules:
  0.0 101.8 jit_solution(8573732677733885689)
XLA Ops:
  0.0 0.0 copy-start
  0.0 0.0 copy-start.1
  0.0 0.0 copy-start.2
  0.0 4.9 %shard_map.46 = f32[1024,128]{1,0:T(8,128)} custom-call(s32[8,7]{1,0:T(8,128)} %gate_qubits.1, s32[9]{0:T(128)} %swap_order.1, f32[1024,128]{1,0:T(8,128)} %bitcast.20, f32[8,2,128,128]{3,2,1,0:T(8,128)} %gates_ref.1), custom_call_target="tpu_custom_call" | custom-call | flops 3000000000 | bytes 1048576 | tf_op jit(solution)/shard_map/pallas_call | solution.py:296
  4.9 24.3 %all-to-all-start = ((f32[512,2,128]{2,1,0:T(2,128)}), f32[512,2,128]{2,1,0:T(2,128)S(1)}, u32[]{:S(2)}, u32[]{:S(2)}) async-start(f32[512,2,128]{2,1,0:T(2,128)} %bitcast.19), calls=%async_computation | async-start | bytes 1048576 | tf_op jit(solution)/shard_map/all_to_all | solution.py:307
  29.3 0.0 copy-done
  29.3 0.0 copy-done.1
  29.3 0.0 copy-done.2
  29.3 10.1 %shard_map.47.matrices_hbm = bf16[4096,512]{1,0:T(8,128)(2,1)S(1)} custom-call(s32[8,7]{1,0:T(8,128)S(1)} %copy-done.1, s32[9]{0:T(128)S(1)} %copy-done.2, f32[8,2,128,128]{3,2,1,0:T(8,128)S(1)} %copy-done), custom_call_target="tpu_custom_call" | custom-call | flops 10000000000 | bytes 1048576 | tf_op jit(solution)/shard_map/pallas_call | solution.py:296
  39.4 0.0 copy-start.3
  39.4 1.9 %copy-done.3 = bf16[4096,512]{1,0:T(8,128)(2,1)} copy-done((bf16[4096,512]{1,0:T(8,128)(2,1)}, bf16[4096,512]{1,0:T(8,128)(2,1)S(1)}, u32[]{:S(2)}) %copy-start.3) | copy-done | bytes 4194328
  41.4 22.8 %all-to-all-done = f32[512,2,128]{2,1,0:T(2,128)S(1)} async-done(((f32[512,2,128]{2,1,0:T(2,128)}), f32[512,2,128]{2,1,0:T(2,128)S(1)}, u32[]{:S(2)}, u32[]{:S(2)}) %all-to-all-start) | async-done | bytes 524320 | tf_op jit(solution)/shard_map/all_to_all | solution.py:307
  64.1 4.1 %shard_map.48 = f32[16,72,128]{2,1,0:T(8,128)S(1)} custom-call(f32[1024,128]{1,0:T(8,128)S(1)} %bitcast.16, bf16[4096,512]{1,0:T(8,128)(2,1)} %copy-done.3), custom_call_target="tpu_custom_call" | custom-call | flops 2000000000 | bytes 1048576 | tf_op jit(solution)/shard_map/pallas_call | solution.py:296
  68.3 15.4 %all_to_all.15.arrived_ref = f32[16,72,128]{2,1,0:T(8,128)S(1)} all-to-all(f32[16,72,128]{2,1,0:T(8,128)S(1)} %shard_map.48), channel_id=1, replica_groups=mesh['z'=16,'x'=4,'core'=2,'narrow'=4] {'x','narrow'}, dimensions={0} | all-to-all | bytes 1179648 | tf_op jit(solution)/shard_map/all_to_all | solution.py:307
  83.7 16.4 %all_to_all.16 = f32[32,1,128]{2,1,0:T(1,128)S(1)} all-to-all(f32[32,1,128]{2,1,0:T(1,128)S(1)} %bitcast.18), channel_id=1, replica_groups=mesh['z'=16,'x'=4,'core'=2,'narrow'=4] {'core','z'}, dimensions={0} | all-to-all | bytes 32768 | tf_op jit(solution)/shard_map/all_to_all | solution.py:307
  100.1 1.7 %shard_map.50 = f32[1024,128]{1,0:T(8,128)} custom-call(f32[32,128]{1,0:T(8,128)S(1)} %bitcast.17, f32[16,72,128]{2,1,0:T(8,128)S(1)} %all_to_all.15.arrived_ref), custom_call_target="tpu_custom_call" | custom-call | flops 10000000 | bytes 1048576 | tf_op jit(solution)/shard_map/pallas_call | solution.py:296
  (1 shorter events, 0.0 us)
Async XLA Ops:
  0.0 29.3 %copy-start = (f32[8,2,128,128]{3,2,1,0:T(8,128)S(1)}, f32[8,2,128,128]{3,2,1,0:T(8,128)}, u32[]{:S(2)}) copy-start(f32[8,2,128,128]{3,2,1,0:T(8,128)} %gates_ref.1) | copy-start | bytes 3145732
  0.0 29.3 %copy-start.1 = (s32[8,7]{1,0:T(8,128)S(1)}, s32[8,7]{1,0:T(8,128)}, u32[]{:S(2)}) copy-start(s32[8,7]{1,0:T(8,128)} %gate_qubits.1) | copy-start | bytes 676
  0.0 29.3 %copy-start.2 = (s32[9]{0:T(128)S(1)}, s32[9]{0:T(128)}, u32[]{:S(2)}) copy-start(s32[9]{0:T(128)} %swap_order.1) | copy-start | bytes 112
  4.9 59.2 %all-to-all-start = ((f32[512,2,128]{2,1,0:T(2,128)}), f32[512,2,128]{2,1,0:T(2,128)S(1)}, u32[]{:S(2)}, u32[]{:S(2)}) async-start(f32[512,2,128]{2,1,0:T(2,128)} %bitcast.19), calls=%async_computation | async-start | bytes 1048576 | tf_op jit(solution)/shard_map/all_to_all | solution.py:307
  39.4 1.9 %copy-start.3 = (bf16[4096,512]{1,0:T(8,128)(2,1)}, bf16[4096,512]{1,0:T(8,128)(2,1)S(1)}, u32[]{:S(2)}) copy-start(bf16[4096,512]{1,0:T(8,128)(2,1)S(1)} %shard_map.47.matrices_hbm) | copy-start | bytes 12582916
